TPU v7x, 32 devices: a whole 2x2x4 slice. The times are simulated.
32 devices in a mesh: dp: 8 (over y, x, core), mp: 4 (over z).
Axes of the slice: x: 2, y: 2, z: 4, core: 2. Of those that a mesh axis runs over, the one named last changes fastest.
Arguments:
- inputs: bfloat16 [32, 512, 768], P('dp', 'mp'), may hold values from -6 to 6
- segment_ids: int32 [32, 512], P('dp'), may hold values from 0 to 3, never falling along the last dimension, each value on 1 to 256 neighbouring positions
- w_query: bfloat16 [768, 768], P('dp', 'mp'), may hold values from -0.21875 to 0.21875
- w_key: bfloat16 [768, 768], P('dp', 'mp'), may hold values from -0.21875 to 0.21875
- w_value: bfloat16 [768, 768], P('dp', 'mp'), may hold values from -0.21875 to 0.21875
- w_output: bfloat16 [768, 768], P('mp', 'dp'), may hold values from -1.75 to 1.75
- w_up: bfloat16 [768, 3072], P('dp', 'mp'), may hold values from -0.21875 to 0.21875
- w_down: bfloat16 [3072, 768], P('mp', 'dp'), may hold values from -0.109375 to 0.109375
- gain_attn: bfloat16 [768], P('dp'), may hold values from 0.5 to 1.5
- gain_ffn: bfloat16 [768], P('dp'), may hold values from 0.5 to 1.5
- cotangent: bfloat16 [32, 512, 768], P('dp', 'mp'), may hold values from -6 to 6
Outputs:
- layer_output: bfloat16 [32, 512, 768], P('dp', 'mp')
- input_grad: bfloat16 [32, 512, 768], P('dp', 'mp')
- grad_query: float32 [768, 768], P('dp', 'mp')
- grad_key: float32 [768, 768], P('dp', 'mp')
- grad_value: float32 [768, 768], P('dp', 'mp')
- grad_output: float32 [768, 768], P('mp', 'dp')
- grad_up: float32 [768, 3072], P('dp', 'mp')
- grad_down: float32 [3072, 768], P('mp', 'dp')
- grad_gain_attn: float32 [768], P('dp')
- grad_gain_ffn: float32 [768], P('dp')
Inputs may be any that keep to these rules, and one draw needn't show every extreme that they name: `segment_ids`: within a row the numbers never fall; each document has 1 to 256 molecules, and one of each row has exactly 256.
All inputs are finite; a program needn't handle non-finite values.
Results may differ from a plain program's by a relative error of at most 0.018.
Values may be sent and summed in bfloat16 or wider, within the bound.
A program may use at most 128 MiB of HBM per device.

v0:
```python
import functools

import jax
import jax.numpy as jnp
from jax import lax
from jax.experimental import pallas as pl
from jax.experimental.pallas import tpu as pltpu
from jax.sharding import PartitionSpec as P

D = 768
HEADS = 12
HEAD = 64
EPS = 1e-05
MESH = pl.DeviceIdType.MESH
BF = jnp.bfloat16
F32 = jnp.float32


def dot(left, right, dims):
    return lax.dot_general(left, right, (dims, ((), ())), preferred_element_type=F32)


def natural(left, right):
    return dot(left, right, ((1,), (0,)))


def against(left, right):
    return dot(left, right, ((1,), (1,)))


def inner(left, right):
    return dot(left, right, ((0,), (0,)))


def norm(values):
    shifted = values - jnp.mean(values, axis=1, keepdims=True)
    scale = lax.rsqrt(jnp.mean(shifted * shifted, axis=1, keepdims=True) + EPS)
    return shifted * scale, scale


def norm_back(grad, xhat, scale, gain):
    e = grad * gain
    back = scale * (
        e - jnp.mean(e, axis=1, keepdims=True) - xhat * jnp.mean(e * xhat, axis=1, keepdims=True)
    )
    return back, jnp.sum(grad * xhat, axis=0)


def columns(w, first, count):
    part = w[:, :, first : first + count]
    return jnp.swapaxes(part, 0, 1).reshape(D, -1)


def row_layer(x, cotangent, segment, weights, gain_attn, gain_ffn):
    length = x.shape[0]
    quarters = weights.shape[1]
    width = D // quarters
    attn, up, down = weights[0], weights[1], weights[2]
    w_query, w_value, w_key, w_out = (columns(attn, i * width, width) for i in range(4))
    w_up, w_down = columns(up, 0, D), columns(down, 0, D)
    x = x.astype(F32)
    xhat_a, scale_a = norm(x)
    normed_a = (xhat_a * gain_attn).astype(BF)
    query, keys, values = (
        natural(normed_a, w).astype(BF).reshape(length, HEADS, HEAD) for w in (w_query, w_key, w_value)
    )
    same = segment[:, None] == segment[None, :]
    scores = jnp.einsum("qhd,khd->hqk", query, keys, preferred_element_type=F32) * HEAD**-0.5
    scores = jnp.where(same[None], scores, -1e30)
    exponent = jnp.exp(scores - jnp.max(scores, axis=2, keepdims=True))
    probs = exponent / jnp.sum(exponent, axis=2, keepdims=True)
    context = jnp.einsum("hqk,khd->qhd", probs.astype(BF), values, preferred_element_type=F32)
    context = context.reshape(length, D).astype(BF)
    middle = x + against(context, w_out)
    xhat_f, scale_f = norm(middle)
    normed_f = (xhat_f * gain_ffn).astype(BF)
    hidden = natural(normed_f, w_up)
    activated, gelu_back = jax.vjp(lambda v: jax.nn.gelu(v, approximate=False), hidden)
    activated = activated.astype(BF)
    output = (middle + against(activated, w_down)).astype(BF)

    grad_down = inner(cotangent, activated)
    grad_hidden = gelu_back(natural(cotangent, w_down))[0].astype(BF)
    grad_up = inner(normed_f, grad_hidden)
    back, grad_gain_ffn = norm_back(against(grad_hidden, w_up), xhat_f, scale_f, gain_ffn)
    grad_middle = cotangent.astype(F32) + back
    grad_attended = grad_middle.astype(BF)
    grad_out = inner(grad_attended, context)
    grad_context = natural(grad_attended, w_out).astype(BF).reshape(length, HEADS, HEAD)
    grad_probs = jnp.einsum("qhd,khd->hqk", grad_context, values, preferred_element_type=F32)
    grad_scores = (
        probs * (grad_probs - jnp.sum(probs * grad_probs, axis=2, keepdims=True))
    ).astype(BF)
    query_grad = jnp.einsum("hqk,khd->qhd", grad_scores, keys, preferred_element_type=F32) * HEAD**-0.5
    key_grad = jnp.einsum("hqk,qhd->khd", grad_scores, query, preferred_element_type=F32) * HEAD**-0.5
    value_grad = jnp.einsum(
        "hqk,qhd->khd", probs.astype(BF), grad_context, preferred_element_type=F32
    )
    query_grad, key_grad, value_grad = (
        g.reshape(length, D).astype(BF) for g in (query_grad, key_grad, value_grad)
    )
    grad_normed_a = (
        against(query_grad, w_query) + against(key_grad, w_key) + against(value_grad, w_value)
    )
    back, grad_gain_attn = norm_back(grad_normed_a, xhat_a, scale_a, gain_attn)
    input_grad = (grad_middle + back).astype(BF)

    def quarter(g, count):
        return g.astype(BF).reshape(D, quarters, count).swapaxes(0, 1)

    grads_attn = jnp.concatenate(
        [
            quarter(g, width)
            for g in (
                inner(normed_a, query_grad),
                inner(normed_a, value_grad),
                inner(normed_a, key_grad),
                grad_out,
            )
        ],
        axis=2,
    )
    grads = jnp.stack([grads_attn, quarter(grad_up, D), quarter(grad_down, D)])
    return output, input_grad, grads, jnp.stack([grad_gain_attn, grad_gain_ffn])


def between(value, first, count):
    lane = lax.broadcasted_iota(jnp.int32, value.shape, 1)
    return jnp.where((lane >= first) & (lane < first + count), value, jnp.zeros_like(value))


def place():
    dp, z = lax.axis_index("dp"), lax.axis_index("mp")
    c, x, y = lax.rem(dp, 2), lax.rem(dp // 2, 2), dp // 4
    return dp, z, c, dp + 2 - 4 * x, dp + 4 - 8 * y, dp + 1 - 2 * c


def send(src, dst, ssem, rsem, device):
    return pltpu.make_async_remote_copy(
        src_ref=src, dst_ref=dst, send_sem=ssem, recv_sem=rsem, device_id=device, device_id_type=MESH
    )


def nearest(z, k):
    inner_place = lax.rem((z + 1) // 2, 2)
    first_two = 1 - k // 2
    base = k + inner_place * first_two * (1 - 2 * k)
    return base + (z // 2) * (3 - 2 * base)


def gain_row(parts_ref, index):
    r = lax.broadcasted_iota(jnp.int32, (128, D), 0)
    col = lax.broadcasted_iota(jnp.int32, (128, D), 1)
    spread = jnp.where(lax.rem(col, 96) == r, 1.0, 0.0).astype(BF)
    total = jnp.zeros((1, D), F32)
    col = lax.broadcasted_iota(jnp.int32, (16, D), 1)
    row = lax.broadcasted_iota(jnp.int32, (16, D), 0)
    for p in range(8):
        full = natural(parts_ref[p], spread)
        keep = (row == index) & (col >= 96 * p) & (col < 96 * (p + 1))
        total = total + jnp.sum(jnp.where(keep, full, 0.0), axis=0, keepdims=True)
    return total


BLOCK = 128
LEN = 512


def block(i):
    return pl.ds(pl.multiple_of(i * BLOCK, BLOCK), BLOCK)


def loop(count, step):
    def body(i, _):
        step(i)
        return 0

    lax.fori_loop(0, count, body, 0)


def layer_kernel(
    x_in, ct_in, seg_ref, wq_ref, wk_ref, wv_ref, wo_ref, wup_ref, wdown_ref, ga_ref, gf_ref,
    total_ref, gain_ref, outs_ref, dxs_ref, wide_ref,
    own, gain_own, gain_all, attn, held, x_ref, ct_ref, out_ref, dx_ref,
    nrm, na_t, nf_t, ct_t, ga_t, qb, kb, vb, cb, lse_ref, bias, mid, acc, act, gp,
    staged, sums, from_core, corner, from_plane, from_z, small, small_z, gain_sum,
    local_sem, held_sem, zs, zr, xs, xr, ys, yr, ds, dr, cs, cr, gs, gr, as_, ar,
    ecs, ecr, eks, ekr, eps, epr, ezs, ezr, egs, egr, egzs, egzr,
):
    dp, z, c, nx, ny, nc = place()
    yx, yx_x, yx_y, yx_d = dp // 2, nx // 2, ny // 2, 3 - dp // 2

    barrier = pltpu.get_barrier_semaphore()
    for i in range(1, 8):
        pl.semaphore_signal(barrier, inc=1, device_id=(lax.rem(dp + i, 8), z), device_id_type=MESH)
    for i in range(1, 4):
        pl.semaphore_signal(barrier, inc=1, device_id=(dp, lax.rem(z + i, 4)), device_id_type=MESH)

    own[0] = jnp.concatenate(
        [wq_ref[...], wv_ref[...], wk_ref[...], wo_ref[...].T], axis=1
    )
    own[1] = wup_ref[...]
    own[2] = wdown_ref[...].T
    gain_own[...] = jnp.zeros_like(gain_own)
    gain_own[0:1, 0:96] = ga_ref[...]
    gain_own[1:2, 0:96] = gf_ref[...]
    pl.semaphore_wait(barrier, 10)

    def rows_start(i, src, dst):
        for j in range(1, 4):
            q = lax.rem(z + j, 4)
            send(src.at[q], dst.at[z], as_.at[i, q], ar.at[i, z], (dp, q)).start()
        pltpu.make_async_copy(src.at[z], dst.at[z], local_sem.at[i]).start()

    def rows_wait(i, src, dst):
        for j in range(1, 4):
            q = lax.rem(z + j, 4)
            cp = send(src.at[q], dst.at[q], as_.at[i, q], ar.at[i, q], (dp, q))
            cp.wait_send()
            cp.wait_recv()
        pltpu.make_async_copy(src.at[z], dst.at[z], local_sem.at[i]).wait()

    def tile(g, q, d):
        return attn.at[q, d] if g == 0 else wide_ref.at[g - 1, q, d]

    def z_copy(g, q, side):
        to = z + (1 if side else -1)
        src = own.at[g] if q is None else tile(g, q, dp)
        q = z if q is None else q
        return send(src, tile(g, q, dp), zs.at[g, q, side], zr.at[g, q], (dp, to))

    def z_pass(g, q):
        origin = z if q is None else q

        @pl.when((origin <= z) & (z < 3))
        def _():
            z_copy(g, q, 1).start()

        @pl.when((origin >= z) & (z > 0))
        def _():
            z_copy(g, q, 0).start()

    def z_done(g, q):
        @pl.when((q <= z) & (z < 3))
        def _():
            z_copy(g, q, 1).wait_send()

        @pl.when((q >= z) & (z > 0))
        def _():
            z_copy(g, q, 0).wait_send()

    def x_copy(g, q, src=None):
        src = tile(g, q, dp) if src is None else src
        return send(src, tile(g, q, dp), xs.at[g, q], xr.at[g, q], (nx, z))

    def y_copy(g, q, src=None):
        src = tile(g, q, dp) if src is None else src
        return send(src, tile(g, q, dp), ys.at[g, q], yr.at[g, q], (ny, z))

    def core_copy(g, q, pos, src=None):
        d = 2 * pos + c
        src = tile(g, q, d) if src is None else src
        return send(src, tile(g, q, d), cs.at[g, q, pos], cr.at[g, q, pos], (nc, z))

    def forward(g, q, along_y):
        src, to = (nx, ny) if along_y else (ny, nx)
        return send(tile(g, q, src), tile(g, q, src), ds.at[g, q], dr.at[g, q], (to, z))

    def own_start(g):
        z_pass(g, None)
        x_copy(g, z, own.at[g]).start()
        y_copy(g, z, own.at[g]).start()
        core_copy(g, z, yx, own.at[g]).start()
        pltpu.make_async_copy(own.at[g], tile(g, z, dp), local_sem.at[4 + g]).start()

    def z_step(g, k):
        q = nearest(z, k)
        send(tile(g, q, dp), tile(g, q, dp), zs.at[g, q, 0], zr.at[g, q], (dp, z)).wait_recv()
        z_pass(g, q)
        x_copy(g, q).start()
        y_copy(g, q).start()
        core_copy(g, q, yx).start()

    def plane_step(g, k):
        q = nearest(z, k)
        x_copy(g, q).wait_recv()

        @pl.when(q < 2)
        def _():
            forward(g, q, True).start()

        core_copy(g, q, yx_x).start()
        y_copy(g, q).wait_recv()

        @pl.when(q >= 2)
        def _():
            forward(g, q, False).start()

        core_copy(g, q, yx_y).start()

    def far_step(g, k):
        q = nearest(z, k)
        d = 2 * yx_d + c
        send(tile(g, q, d), tile(g, q, d), ds.at[g, q], dr.at[g, q], (nx, z)).wait_recv()
        core_copy(g, q, yx_d).start()

    def core_ready(g, q):
        for pos in range(4):
            d = 2 * pos + 1 - c
            send(
                tile(g, q, d), tile(g, q, d), cs.at[g, q, pos], cr.at[g, q, pos], (nc, z)
            ).wait_recv()

    def weights_sent(g):
        def step(q):
            z_done(g, q)
            x_copy(g, q).wait_send()
            y_copy(g, q).wait_send()

            @pl.when(q < 2)
            def _():
                forward(g, q, True).wait_send()

            @pl.when(q >= 2)
            def _():
                forward(g, q, False).wait_send()

            for pos in range(4):
                core_copy(g, q, pos).wait_send()

        loop(4, step)

    def own_ready(g):
        pltpu.make_async_copy(own.at[g], tile(g, z, dp), local_sem.at[4 + g]).wait()

    def hold(g, q, slot):
        return pltpu.make_async_copy(wide_ref.at[g - 1, q], held.at[slot], held_sem.at[slot])

    def out_core(g, q):
        return send(staged.at[q], from_core.at[g, q], ecs.at[g, q], ecr.at[g, q], (nc, z))

    def out_corner(g, q):
        to = nx + (ny - nx) * (q // 2)
        return send(sums.at[g, q, yx_d], corner.at[g, q], eks.at[g, q], ekr.at[g, q], (to, z))

    def out_plane(g, q, side):
        to = nx + (ny - nx) * side
        pos = yx_x + (yx_y - yx_x) * side
        return send(
            sums.at[g, q, pos], from_plane.at[g, q, side], eps.at[g, q, side], epr.at[g, q, side], (to, z)
        )

    def out_z(g, q):
        return send(sums.at[g, q, yx], from_z.at[g, z], ezs.at[g, q], ezr.at[g, z], (dp, q))

    def core_add(g, q):
        out_core(g, q).wait_recv()

        def step(pos):
            sums[g, q, pos] = (
                sums[g, q, pos].astype(F32) + from_core[g, q, pos].astype(F32)
            ).astype(BF)

        loop(4, step)
        out_corner(g, q).start()
        out_plane(g, q, q // 2).start()

    def corner_add(g, q):
        side = 1 - q // 2
        pos = yx_x + (yx_y - yx_x) * side
        out_corner(g, q).wait_recv()
        sums[g, q, pos] = (sums[g, q, pos].astype(F32) + corner[g, q].astype(F32)).astype(BF)
        out_plane(g, q, side).start()

    def plane_add(g, q):
        out_plane(g, q, 0).wait_recv()
        out_plane(g, q, 1).wait_recv()
        sums[g, q, yx] = (
            sums[g, q, yx].astype(F32)
            + from_plane[g, q, 0].astype(F32)
            + from_plane[g, q, 1].astype(F32)
        ).astype(BF)

        @pl.when(z != q)
        def _():
            out_z(g, q).start()

    def last_add(g):
        total = sums[g, z, yx].astype(F32)
        for j in range(1, 4):
            q = lax.rem(z + j, 4)
            send(sums.at[g, q, yx], from_z.at[g, q], ezs.at[g, q], ezr.at[g, q], (dp, q)).wait_recv()
            total = total + from_z[g, q].astype(F32)
        total_ref[g] = total

    def grads_sent(g):
        def step(q):
            out_corner(g, q).wait_send()
            out_plane(g, q, 0).wait_send()
            out_plane(g, q, 1).wait_send()

            @pl.when(z != q)
            def _():
                out_z(g, q).wait_send()

        loop(4, step)

    def emit(g, q, left, right, left_2=None, right_2=None):
        if g < 2:
            out_core(g + 1, q).wait_send()
        for other in (True, False):
            half = 1 - c if other else c
            dst = staged.at[q] if other else sums.at[g, q]
            v = natural(left[:, half].reshape(384, LEN), right)
            if right_2 is None:
                dst[...] = v.astype(BF).reshape(4, 96, D)
            else:
                v2 = natural(left_2[:, half].reshape(384, LEN), right_2)
                dst[:, :, 0:512] = v[:, 0:512].astype(BF).reshape(4, 96, 512)
                dst[:, :, 512:640] = (v[:, 512:640] + v2[:, 0:128]).astype(BF).reshape(4, 96, 128)
                dst[:, :, 640:768] = v2[:, 128:256].astype(BF).reshape(4, 96, 128)
            if other:
                out_core(g, q).start()

    def put_t(dst, i, v):
        dst[:, :, :, block(i)] = v.T.reshape(4, 2, 96, BLOCK)

    def add(i, value):
        @pl.when(i == 0)
        def _():
            acc[...] = value

        @pl.when(i > 0)
        def _():
            acc[...] += value

    own_start(0)
    for i in range(1, 8):
        to = lax.rem(dp + i, 8)
        send(gain_own, gain_all.at[dp], gs.at[to], gr.at[dp], (to, z)).start()
    gain_all[dp] = gain_own[...]
    loop(3, lambda k: z_step(0, k + 1))
    rows_start(0, x_in, x_ref)
    own_start(1)
    seg_row = seg_ref[pl.ds(z, 1)].astype(F32)
    seg_col = jnp.broadcast_to(seg_row, (8, LEN)).T[:, 0:1]
    bias[...] = jnp.where(seg_col == seg_row, 0.0, -1e30)
    gain_sum[...] = jnp.zeros_like(gain_sum)
    loop(4, lambda k: plane_step(0, k))
    loop(3, lambda k: z_step(1, k + 1))
    own_start(2)
    for i in range(1, 8):
        other = lax.rem(dp + i, 8)
        send(gain_own, gain_all.at[other], gs.at[other], gr.at[other], (other, z)).wait_recv()
    gain_a = gain_row(gain_all, 0)
    gain_f = gain_row(gain_all, 1)
    loop(4, lambda k: far_step(0, k))
    rows_wait(0, x_in, x_ref)

    def norm_a(i):
        xhat, _ = norm(x_ref[i].astype(F32))
        normed = (xhat * gain_a).astype(BF)
        nrm[block(i)] = normed
        put_t(na_t, i, normed)

    loop(4, norm_a)
    own_ready(0)

    def attend(i):
        q = nearest(z, i)
        core_ready(0, q)
        w = attn[q].reshape(D, D)
        p = natural(nrm[...], w[:, 0:640])
        q8 = p[:, 0:256].astype(BF) * jnp.asarray(0.125, BF)
        v = p[:, 128:384].astype(BF)
        k = p[:, 384:640].astype(BF)
        qb[q] = q8
        vb[q] = v
        kb[q] = k
        for h in range(3):
            for r in range(2):
                rs = slice(256 * r, 256 * (r + 1))
                s = against(between(q8[rs], 64 * h, 64), k) + bias[rs]
                m = jnp.max(s, axis=1, keepdims=True)
                e = jnp.exp(s - m)
                total = jnp.sum(e, axis=1, keepdims=True)
                probs = (e * (1.0 / total)).astype(BF)
                part = between(natural(probs, v), 64 + 64 * h, 64).astype(BF)
                if h == 0:
                    cb[q, rs] = part
                else:
                    cb[q, rs] += part
                lane = lax.broadcasted_iota(jnp.int32, (256, 128), 1)
                lse_ref[rs] = jnp.where(lane == 3 * q + h, m + jnp.log(total), lse_ref[rs])
            if h == 0:
                plane_step(1, i)
            if h == 1:
                @pl.when(i < 3)
                def _():
                    z_step(2, i + 1)

    loop(4, attend)
    rows_start(1, ct_in, ct_ref)

    def attend_out(i):
        add(i, against(cb[i], attn[i].reshape(D, D)[:, 512:768]))
        far_step(1, i)

    loop(4, attend_out)
    own_ready(1)

    def norm_f(i):
        m = x_ref[i].astype(F32) + acc[block(i)]
        mid[block(i)] = m
        xhat, _ = norm(m)
        normed = (xhat * gain_f).astype(BF)
        nrm[block(i)] = normed
        put_t(nf_t, i, normed)

    loop(4, norm_f)
    q = nearest(z, 0)
    core_ready(1, q)
    hold(1, q, 0).start()

    def up(i):
        q = nearest(z, i)
        slot = lax.rem(i, 2)

        @pl.when(i < 3)
        def _():
            later = nearest(z, i + 1)
            core_ready(1, later)
            hold(1, later, 1 - slot).start()

        hold(1, q, slot).wait()
        w = held[slot].reshape(D, D)
        for r in range(2):
            rs = slice(256 * r, 256 * (r + 1))
            h = natural(nrm[rs], w)
            cdf = 0.5 + 0.5 * lax.erf(h * 0.7071067811865476)
            act[q, rs] = (h * cdf).astype(BF)
            gp[q, rs] = (cdf + h * (jnp.exp(-0.5 * h * h) * 0.3989422804014327)).astype(BF)
        plane_step(2, i)

    loop(4, up)
    rows_wait(1, ct_in, ct_ref)

    def turn_ct(i):
        put_t(ct_t, i, ct_ref[i])
        far_step(2, i)

    loop(4, turn_ct)
    own_ready(2)

    def grad_down(i):
        emit(2, i, ct_t, act[i])

        @pl.when(i > 0)
        def _():
            core_add(2, i - 1)

    loop(4, grad_down)
    core_add(2, 3)
    q = nearest(z, 0)
    core_ready(2, q)
    hold(2, q, 0).start()

    def down(i):
        q = nearest(z, i)
        slot = lax.rem(i, 2)

        @pl.when(i < 3)
        def _():
            later = nearest(z, i + 1)
            core_ready(2, later)
            hold(2, later, 1 - slot).start()

        hold(2, q, slot).wait()
        w = held[slot].reshape(D, D)
        gp[q] = (natural(ct_ref[...].reshape(LEN, D), w) * gp[q].astype(F32)).astype(BF)
        add(i, against(act[q], w))

    loop(4, down)
    hold(1, 0, 0).start()
    out_ref[...] = (mid[...] + acc[...]).astype(BF).reshape(4, BLOCK, D)
    rows_start(2, out_ref, outs_ref)
    loop(4, lambda k: corner_add(2, k))

    def up_back(i):
        slot = lax.rem(i, 2)

        @pl.when(i < 3)
        def _():
            hold(1, i + 1, 1 - slot).start()

        hold(1, i, slot).wait()
        add(i, against(gp[i], held[slot].reshape(D, D)))
        emit(1, i, nf_t, gp[i])

        @pl.when(i > 0)
        def _():
            core_add(1, i - 1)

    loop(4, up_back)
    core_add(1, 3)

    def norm_f_back(i):
        xhat, scale = norm(mid[block(i)])
        back, grad_gain = norm_back(acc[block(i)], xhat, scale, gain_f)
        gain_sum[1:2] += grad_gain[None]
        grad_middle = ct_ref[i].astype(F32) + back
        mid[block(i)] = grad_middle
        attended = grad_middle.astype(BF)
        nrm[block(i)] = attended
        put_t(ga_t, i, attended)

    loop(4, norm_f_back)

    def attend_back(i):
        w = attn[i].reshape(D, D)
        dctx = between(natural(nrm[...], w[:, 512:768]), 64, 192).astype(BF)
        q8, v, k, cx = qb[i], vb[i], kb[i], cb[i]
        dq = jnp.zeros((LEN, 256), F32)
        dk = jnp.zeros((LEN, 256), F32)
        dv = jnp.zeros((LEN, 256), F32)
        for h in range(3):
            lane = lax.broadcasted_iota(jnp.int32, (LEN, 128), 1)
            lse = jnp.sum(jnp.where(lane == 3 * i + h, lse_ref[...], 0.0), axis=1, keepdims=True)
            p = jnp.exp(against(between(q8, 64 * h, 64), k) + bias[...] - lse)
            dm = between(dctx, 64 + 64 * h, 64)
            delta = jnp.sum(dm.astype(F32) * cx.astype(F32), axis=1, keepdims=True)
            ds_ = (p * (against(dm, v) - delta)).astype(BF)
            dq += between(natural(ds_, k), 64 * h, 64)
            dk += between(inner(ds_, q8), 64 * h, 64)
            dv += between(inner(p.astype(BF), dctx), 64 + 64 * h, 64)
            if h == 0:
                plane_add(2, i)
            if h == 1:
                corner_add(1, i)
        dq = dq * 0.125
        d = jnp.concatenate(
            [dq[:, 0:128], dq[:, 128:256] + dv[:, 0:128], dv[:, 128:256], dk], axis=1
        ).astype(BF)
        add(i, against(d, w[:, 0:640]))
        emit(0, i, na_t, d, ga_t, cx)

        @pl.when(i > 0)
        def _():
            core_add(0, i - 1)

    loop(4, attend_back)
    core_add(0, 3)

    def norm_a_back(i):
        xhat, scale = norm(x_ref[i].astype(F32))
        back, grad_gain = norm_back(acc[block(i)], xhat, scale, gain_a)
        gain_sum[0:1] += grad_gain[None]
        dx_ref[i] = (mid[block(i)] + back).astype(BF)

    loop(4, norm_a_back)
    rows_start(3, dx_ref, dxs_ref)
    last_add(2)

    def small_copy(i):
        return send(gain_sum, small.at[i], egs.at[i], egr.at[i], ((nc, nx, ny)[i], z))

    def small_add(i):
        small_copy(i).wait()
        gain_sum[...] += small[i]

    small_copy(0).start()
    loop(4, lambda k: corner_add(0, k))
    small_add(0)
    small_copy(1).start()
    loop(4, lambda k: plane_add(1, k))
    small_add(1)
    small_copy(2).start()
    last_add(1)
    small_add(2)
    for j in range(1, 4):
        q = lax.rem(z + j, 4)
        send(gain_sum, small_z.at[z], egzs.at[q], egzr.at[z], (dp, q)).start()
    loop(4, lambda k: plane_add(0, k))
    total = gain_sum[...]
    for j in range(1, 4):
        q = lax.rem(z + j, 4)
        cp = send(gain_sum, small_z.at[q], egzs.at[q], egzr.at[q], (dp, q))
        cp.wait()
        total = total + small_z[q]
    gain_ref[...] = total
    last_add(0)

    for i in range(1, 8):
        other = lax.rem(dp + i, 8)
        send(gain_own, gain_all.at[other], gs.at[other], gr.at[other], (other, z)).wait_send()
    for g in range(3):
        weights_sent(g)
        grads_sent(g)
    loop(4, lambda q: out_core(0, q).wait_send())
    rows_wait(2, out_ref, outs_ref)
    rows_wait(3, dx_ref, dxs_ref)


def layer(x, ct, segment_ids, w_query, w_key, w_value, w_output, w_up, w_down, gain_attn, gain_ffn):
    sem = pltpu.SemaphoreType.DMA
    vm = pltpu.VMEM
    anywhere = pl.BlockSpec(memory_space=pl.ANY)
    vmem = pl.BlockSpec(memory_space=pltpu.VMEM)
    return pl.pallas_call(
        layer_kernel,
        out_shape=(
            jax.ShapeDtypeStruct((3, 96, D), F32),
            jax.ShapeDtypeStruct((8, D), F32),
            jax.ShapeDtypeStruct(x.shape, BF),
            jax.ShapeDtypeStruct(x.shape, BF),
            jax.ShapeDtypeStruct((2, 4, 8, 96, D), BF),
        ),
        in_specs=[anywhere] * 2 + [vmem] * 9,
        out_specs=(vmem, vmem, anywhere, anywhere, anywhere),
        scratch_shapes=[
            vm((3, 96, D), BF), vm((16, 128), BF), vm((8, 16, 128), BF),
            vm((4, 8, 96, D), BF), vm((2, 8, 96, D), BF),
            vm((4, BLOCK, D), BF), vm((4, BLOCK, D), BF), vm((4, BLOCK, D), BF), vm((4, BLOCK, D), BF),
            vm((LEN, D), BF),
            vm((4, 2, 96, LEN), BF), vm((4, 2, 96, LEN), BF), vm((4, 2, 96, LEN), BF), vm((4, 2, 96, LEN), BF),
            vm((4, LEN, 256), BF), vm((4, LEN, 256), BF), vm((4, LEN, 256), BF), vm((4, LEN, 256), BF),
            vm((LEN, 128), F32), vm((LEN, LEN), F32), vm((LEN, D), F32), vm((LEN, D), F32),
            vm((4, LEN, D), BF), vm((4, LEN, D), BF),
            vm((4, 4, 96, D), BF), vm((3, 4, 4, 96, D), BF), vm((3, 4, 4, 96, D), BF),
            vm((3, 4, 96, D), BF), vm((3, 4, 2, 96, D), BF), vm((3, 4, 96, D), BF),
            vm((3, 8, D), F32), vm((4, 8, D), F32), vm((8, D), F32),
            sem((7,)), sem((2,)),
            sem((3, 4, 2)), sem((3, 4)),
            sem((3, 4)), sem((3, 4)),
            sem((3, 4)), sem((3, 4)),
            sem((3, 4)), sem((3, 4)),
            sem((3, 4, 4)), sem((3, 4, 4)),
            sem((8,)), sem((8,)),
            sem((4, 4)), sem((4, 4)),
            sem((3, 4)), sem((3, 4)),
            sem((3, 4)), sem((3, 4)),
            sem((3, 4, 2)), sem((3, 4, 2)),
            sem((3, 4)), sem((3, 4)),
            sem((3,)), sem((3,)),
            sem((4,)), sem((4,)),
        ],
        compiler_params=pltpu.CompilerParams(
            collective_id=0, has_side_effects=True, vmem_limit_bytes=VMEM_LIMIT
        ),
        name="layer_with_copies",
    )(x, ct, segment_ids, w_query, w_key, w_value, w_output, w_up, w_down, gain_attn, gain_ffn)


VMEM_LIMIT = 62 * 2**20


def shards(
    inputs, segment_ids, w_query, w_key, w_value, w_output, w_up, w_down, gain_attn, gain_ffn, cotangent,
    *, parts, quarters,
):
    depth, width = w_query.shape
    index = lax.axis_index("dp")
    if parts == 8 and quarters == 4:
        total, gg, out, dx, _ = layer(
            inputs, cotangent, segment_ids, w_query, w_key, w_value, w_output, w_up, w_down,
            gain_attn.reshape(1, depth), gain_ffn.reshape(1, depth),
        )
        gg = lax.dynamic_slice_in_dim(gg, index * depth, depth, 1)
    else:
        z = lax.axis_index("mp")
        segment = lax.dynamic_index_in_dim(segment_ids, z, 0, keepdims=False)
        own = jnp.stack(
            [jnp.concatenate([w_query, w_value, w_key, w_output.T], axis=1), w_up, w_down.T]
        )
        weights = lax.all_gather(own, ("dp", "mp"), axis=0).reshape(parts, quarters, 3, depth, D)
        weights = weights.transpose(2, 1, 0, 3, 4).reshape(3, quarters, D, D)
        gains = jnp.stack(
            [lax.all_gather(g, "dp", axis=0, tiled=True) for g in (gain_attn, gain_ffn)]
        ).astype(F32)
        x, ct = (
            lax.all_to_all(a, "mp", split_axis=0, concat_axis=0, tiled=True) for a in (inputs, cotangent)
        )
        out, dx, grads, gg = row_layer(
            x.reshape(-1, D), ct.reshape(-1, D), segment, weights, gains[0], gains[1]
        )
        grads = grads.reshape(3, quarters, parts, depth, D).transpose(2, 1, 0, 3, 4)
        grads = grads.reshape(parts * quarters, 3, depth, D)
        total = lax.psum_scatter(grads, ("dp", "mp"), scatter_dimension=0).astype(F32)
        gg = lax.psum(lax.psum_scatter(gg, "dp", scatter_dimension=1, tiled=True), "mp")
        out, dx = (
            lax.all_to_all(a.reshape(inputs.shape), "mp", split_axis=0, concat_axis=0, tiled=True)
            for a in (out, dx)
        )
    return (
        out,
        dx,
        total[0, :, :width],
        total[0, :, 2 * width : 3 * width],
        total[0, :, width : 2 * width],
        total[0, :, 3 * width :].T,
        total[1],
        total[2].T,
        gg[0],
        gg[1],
    )


def solution(mesh):
    by_row = P("dp", "mp", None)
    grids = (P("dp", "mp"), P("dp", "mp"), P("dp", "mp"), P("mp", "dp"), P("dp", "mp"), P("mp", "dp"))
    gains = (P("dp"), P("dp"))
    return jax.shard_map(
        functools.partial(shards, parts=mesh.shape["dp"], quarters=mesh.shape["mp"]),
        mesh=mesh,
        in_specs=(by_row, P("dp", None)) + grids + gains + (by_row,),
        out_specs=(by_row, by_row) + grids + gains,
        check_vma=False,
    )
```

profile of v0, /device:TPU:0, one launch (start us, length us, event | category | flops | bytes accessed | tf_op | source)
XLA Modules:
  0.0 204.4 jit_solution(13844612423292422747)
XLA Ops:
  0.6 1.7 copy.21.wdown_ref
  2.4 192.1 %layer_with_copies.1 = (f32[3,96,768]{2,1,0:T(8,128)}, f32[8,768]{1,0:T(8,128)}, bf16[4,128,768]{2,1,0:T(8,128)(2,1)}, bf16[4,128,768]{2,1,0:T(8,128)(2,1)}, bf16[2,4,8,96,768]{4,3,2,1,0:T(8,128)(2,1)}) custom-call(bf16[4,128,768]{2,1,0:T(8,128)(2,1)} %x_in.1, bf16[4,128,768]{2,1,0:T(8,128)(2,1)} %ct_in.1, s32[4,512]{1,0:T(4,128)} %seg_ref.1, ...), custom_call_target="tpu_custom_call" | custom-call | tf_op jit(solution)/shard_map/layer_with_copies/pallas_call | solution.py:709
  194.5 1.8 slice_bitcast_fusion.2
  196.3 0.7 copy.22
  197.1 1.9 slice_bitcast_fusion
  199.0 0.8 constant_dynamic-slice_fusion
  199.7 0.5 slice_bitcast_fusion.6
  200.3 2.1 %copy.25 = bf16[4,128,768]{2,1,0:T(8,128)(2,1)} copy(bf16[4,128,768]{2,1,0:T(8,128)(2,1)} %get-tuple-element.46) | data formatting | bytes 1572864
  202.3 2.1 %copy.26 = bf16[4,128,768]{2,1,0:T(8,128)(2,1)} copy(bf16[4,128,768]{2,1,0:T(8,128)(2,1)} %get-tuple-element.47) | data formatting | bytes 1572864
where the time goes:
time: 207 us; the launch traced here: 204 us
  Pallas kernels  192 us (93%)
  local copies, waits for them, and re-layouts  11.6 us (6%)
    pallas_call x1, Pallas kernels, layer(): pl.pallas_call(layer_kernel, out_shape=(jax.ShapeDtypeStruct((3, 96, D),...  192 us
    unnamed x4, local copies, waits for them, and re-layouts  6.59 us

commit v1 on v0

--- a/solution.py
+++ b/solution.py
@@ -183,7 +183,7 @@
     total_ref, gain_ref, outs_ref, dxs_ref, wide_ref,
     own, gain_own, gain_all, attn, held, x_ref, ct_ref, out_ref, dx_ref,
     nrm, na_t, nf_t, ct_t, ga_t, qb, kb, vb, cb, lse_ref, bias, mid, acc, act, gp,
-    staged, sums, from_core, corner, from_plane, from_z, small, small_z, gain_sum,
+    staged, sums, from_core, corner, from_plane, from_z, small, small_z, gain_sum, gain_parts,
     local_sem, held_sem, zs, zr, xs, xr, ys, yr, ds, dr, cs, cr, gs, gr, as_, ar,
     ecs, ecr, eks, ekr, eps, epr, ezs, ezr, egs, egr, egzs, egzr,
 ):
@@ -200,7 +200,7 @@
         [wq_ref[...], wv_ref[...], wk_ref[...], wo_ref[...].T], axis=1
     )
     own[1] = wup_ref[...]
-    own[2] = wdown_ref[...].T
+    own[2] = wdown_ref[...]
     gain_own[...] = jnp.zeros_like(gain_own)
     gain_own[0:1, 0:96] = ga_ref[...]
     gain_own[1:2, 0:96] = gf_ref[...]
@@ -285,14 +285,14 @@
         q = nearest(z, k)
         x_copy(g, q).wait_recv()
 
-        @pl.when(q < 2)
+        @pl.when(lax.rem(q, 2) == 0)
         def _():
             forward(g, q, True).start()
 
         core_copy(g, q, yx_x).start()
         y_copy(g, q).wait_recv()
 
-        @pl.when(q >= 2)
+        @pl.when(lax.rem(q, 2) == 1)
         def _():
             forward(g, q, False).start()
 
@@ -317,11 +317,11 @@
             x_copy(g, q).wait_send()
             y_copy(g, q).wait_send()
 
-            @pl.when(q < 2)
+            @pl.when(lax.rem(q, 2) == 0)
             def _():
                 forward(g, q, True).wait_send()
 
-            @pl.when(q >= 2)
+            @pl.when(lax.rem(q, 2) == 1)
             def _():
                 forward(g, q, False).wait_send()
 
@@ -340,7 +340,7 @@
         return send(staged.at[q], from_core.at[g, q], ecs.at[g, q], ecr.at[g, q], (nc, z))
 
     def out_corner(g, q):
-        to = nx + (ny - nx) * (q // 2)
+        to = nx + (ny - nx) * lax.rem(q, 2)
         return send(sums.at[g, q, yx_d], corner.at[g, q], eks.at[g, q], ekr.at[g, q], (to, z))
 
     def out_plane(g, q, side):
@@ -363,10 +363,17 @@
 
         loop(4, step)
         out_corner(g, q).start()
-        out_plane(g, q, q // 2).start()
+
+        @pl.when(q >= 2)
+        def _():
+            out_plane(g, q - 2, lax.rem(q, 2)).start()
 
     def corner_add(g, q):
-        side = 1 - q // 2
+        @pl.when(q < 2)
+        def _():
+            out_plane(g, q + 2, lax.rem(q, 2)).start()
+
+        side = 1 - lax.rem(q, 2)
         pos = yx_x + (yx_y - yx_x) * side
         out_corner(g, q).wait_recv()
         sums[g, q, pos] = (sums[g, q, pos].astype(F32) + corner[g, q].astype(F32)).astype(BF)
@@ -439,21 +446,25 @@
         to = lax.rem(dp + i, 8)
         send(gain_own, gain_all.at[dp], gs.at[to], gr.at[dp], (to, z)).start()
     gain_all[dp] = gain_own[...]
+    own_start(1)
     loop(3, lambda k: z_step(0, k + 1))
+    loop(3, lambda k: z_step(1, k + 1))
+    own_start(2)
+    loop(4, lambda k: plane_step(0, k))
     rows_start(0, x_in, x_ref)
-    own_start(1)
     seg_row = seg_ref[pl.ds(z, 1)].astype(F32)
     seg_col = jnp.broadcast_to(seg_row, (8, LEN)).T[:, 0:1]
     bias[...] = jnp.where(seg_col == seg_row, 0.0, -1e30)
     gain_sum[...] = jnp.zeros_like(gain_sum)
-    loop(4, lambda k: plane_step(0, k))
-    loop(3, lambda k: z_step(1, k + 1))
-    own_start(2)
+    gain_parts[...] = jnp.zeros_like(gain_parts)
     for i in range(1, 8):
         other = lax.rem(dp + i, 8)
         send(gain_own, gain_all.at[other], gs.at[other], gr.at[other], (other, z)).wait_recv()
     gain_a = gain_row(gain_all, 0)
     gain_f = gain_row(gain_all, 1)
+    loop(3, lambda k: z_step(2, k + 1))
+    rows_start(1, ct_in, ct_ref)
+    loop(4, lambda k: plane_step(1, k))
     loop(4, lambda k: far_step(0, k))
     rows_wait(0, x_in, x_ref)
 
@@ -493,18 +504,14 @@
                 lane = lax.broadcasted_iota(jnp.int32, (256, 128), 1)
                 lse_ref[rs] = jnp.where(lane == 3 * q + h, m + jnp.log(total), lse_ref[rs])
             if h == 0:
-                plane_step(1, i)
-            if h == 1:
-                @pl.when(i < 3)
-                def _():
-                    z_step(2, i + 1)
+                far_step(1, i)
+            if h == 2:
+                plane_step(2, i)
 
     loop(4, attend)
-    rows_start(1, ct_in, ct_ref)
 
     def attend_out(i):
         add(i, against(cb[i], attn[i].reshape(D, D)[:, 512:768]))
-        far_step(1, i)
 
     loop(4, attend_out)
     own_ready(1)
@@ -540,14 +547,13 @@
             cdf = 0.5 + 0.5 * lax.erf(h * 0.7071067811865476)
             act[q, rs] = (h * cdf).astype(BF)
             gp[q, rs] = (cdf + h * (jnp.exp(-0.5 * h * h) * 0.3989422804014327)).astype(BF)
-        plane_step(2, i)
+        far_step(2, i)
 
     loop(4, up)
     rows_wait(1, ct_in, ct_ref)
 
     def turn_ct(i):
         put_t(ct_t, i, ct_ref[i])
-        far_step(2, i)
 
     loop(4, turn_ct)
     own_ready(2)
@@ -579,12 +585,12 @@
         w = held[slot].reshape(D, D)
         gp[q] = (natural(ct_ref[...].reshape(LEN, D), w) * gp[q].astype(F32)).astype(BF)
         add(i, against(act[q], w))
+        corner_add(2, i)
 
     loop(4, down)
     hold(1, 0, 0).start()
     out_ref[...] = (mid[...] + acc[...]).astype(BF).reshape(4, BLOCK, D)
     rows_start(2, out_ref, outs_ref)
-    loop(4, lambda k: corner_add(2, k))
 
     def up_back(i):
         slot = lax.rem(i, 2)
@@ -634,9 +640,20 @@
             dk += between(inner(ds_, q8), 64 * h, 64)
             dv += between(inner(p.astype(BF), dctx), 64 + 64 * h, 64)
             if h == 0:
-                plane_add(2, i)
+                @pl.when(i < 2)
+                def _():
+                    plane_add(2, 2 * i)
+                    plane_add(2, 2 * i + 1)
             if h == 1:
-                corner_add(1, i)
+                @pl.when(i < 2)
+                def _():
+                    corner_add(1, 2 * i)
+                    corner_add(1, 2 * i + 1)
+
+                @pl.when(i >= 2)
+                def _():
+                    plane_add(1, 2 * i - 4)
+                    plane_add(1, 2 * i - 3)
         dq = dq * 0.125
         d = jnp.concatenate(
             [dq[:, 0:128], dq[:, 128:256] + dv[:, 0:128], dv[:, 128:256], dk], axis=1
@@ -659,35 +676,42 @@
 
     loop(4, norm_a_back)
     rows_start(3, dx_ref, dxs_ref)
-    last_add(2)
 
     def small_copy(i):
-        return send(gain_sum, small.at[i], egs.at[i], egr.at[i], ((nc, nx, ny)[i], z))
+        return send(gain_parts, small.at[i], egs.at[i], egr.at[i], ((nc, nx, ny)[i], z))
 
     def small_add(i):
         small_copy(i).wait()
-        gain_sum[...] += small[i]
-
+        gain_parts[...] += small[i]
+
+    for i in range(2):
+        for p in range(8):
+            gain_parts[8 * i + p : 8 * i + p + 1, 0:96] = gain_sum[i : i + 1, 96 * p : 96 * (p + 1)]
     small_copy(0).start()
-    loop(4, lambda k: corner_add(0, k))
+    corner_add(0, 0)
     small_add(0)
     small_copy(1).start()
-    loop(4, lambda k: plane_add(1, k))
+    corner_add(0, 1)
+    corner_add(0, 2)
     small_add(1)
     small_copy(2).start()
+    corner_add(0, 3)
+    last_add(2)
     last_add(1)
     small_add(2)
     for j in range(1, 4):
         q = lax.rem(z + j, 4)
-        send(gain_sum, small_z.at[z], egzs.at[q], egzr.at[z], (dp, q)).start()
+        send(gain_parts, small_z.at[z], egzs.at[q], egzr.at[z], (dp, q)).start()
     loop(4, lambda k: plane_add(0, k))
-    total = gain_sum[...]
+    total = gain_parts[...]
     for j in range(1, 4):
         q = lax.rem(z + j, 4)
-        cp = send(gain_sum, small_z.at[q], egzs.at[q], egzr.at[q], (dp, q))
+        cp = send(gain_parts, small_z.at[q], egzs.at[q], egzr.at[q], (dp, q))
         cp.wait()
         total = total + small_z[q]
-    gain_ref[...] = total
+    gain_parts[...] = total
+    gain_ref[0:1] = gain_parts[pl.ds(dp, 1)]
+    gain_ref[1:2] = gain_parts[pl.ds(dp + 8, 1)]
     last_add(0)
 
     for i in range(1, 8):
@@ -710,7 +734,7 @@
         layer_kernel,
         out_shape=(
             jax.ShapeDtypeStruct((3, 96, D), F32),
-            jax.ShapeDtypeStruct((8, D), F32),
+            jax.ShapeDtypeStruct((8, 128), F32),
             jax.ShapeDtypeStruct(x.shape, BF),
             jax.ShapeDtypeStruct(x.shape, BF),
             jax.ShapeDtypeStruct((2, 4, 8, 96, D), BF),
@@ -728,7 +752,7 @@
             vm((4, LEN, D), BF), vm((4, LEN, D), BF),
             vm((4, 4, 96, D), BF), vm((3, 4, 4, 96, D), BF), vm((3, 4, 4, 96, D), BF),
             vm((3, 4, 96, D), BF), vm((3, 4, 2, 96, D), BF), vm((3, 4, 96, D), BF),
-            vm((3, 8, D), F32), vm((4, 8, D), F32), vm((8, D), F32),
+            vm((3, 16, 128), F32), vm((4, 16, 128), F32), vm((8, D), F32), vm((16, 128), F32),
             sem((7,)), sem((2,)),
             sem((3, 4, 2)), sem((3, 4)),
             sem((3, 4)), sem((3, 4)),
@@ -754,18 +778,47 @@
 VMEM_LIMIT = 62 * 2**20
 
 
+def part_kernel(
+    total_ref, gain_ref, out_ref, dx_ref,
+    outs_ref, dxs_ref, q_ref, k_ref, v_ref, o_ref, up_ref, down_ref, ga_ref, gf_ref,
+):
+    outs_ref[...] = out_ref[...]
+    dxs_ref[...] = dx_ref[...]
+    attn = total_ref[0]
+    q_ref[...] = attn[:, 0:192]
+    v_ref[...] = attn[:, 192:384]
+    k_ref[...] = attn[:, 384:576]
+    o_ref[...] = attn[:, 576:768].T
+    up_ref[...] = total_ref[1]
+    down_ref[...] = total_ref[2]
+    ga_ref[...] = gain_ref[0:1, 0:96]
+    gf_ref[...] = gain_ref[1:2, 0:96]
+
+
+def part(total, gain, out, dx):
+    vmem = pl.BlockSpec(memory_space=pltpu.VMEM)
+    shapes = [(96, 192)] * 3 + [(192, 96), (96, D), (96, D), (1, 96), (1, 96)]
+    return pl.pallas_call(
+        part_kernel,
+        out_shape=[jax.ShapeDtypeStruct(out.shape, BF)] * 2 + [jax.ShapeDtypeStruct(n, F32) for n in shapes],
+        in_specs=[vmem] * 4,
+        out_specs=[vmem] * 10,
+        name="part_outputs",
+    )(total, gain, out, dx)
+
+
 def shards(
     inputs, segment_ids, w_query, w_key, w_value, w_output, w_up, w_down, gain_attn, gain_ffn, cotangent,
     *, parts, quarters,
 ):
     depth, width = w_query.shape
-    index = lax.axis_index("dp")
     if parts == 8 and quarters == 4:
         total, gg, out, dx, _ = layer(
-            inputs, cotangent, segment_ids, w_query, w_key, w_value, w_output, w_up, w_down,
+            inputs, cotangent, segment_ids, w_query, w_key, w_value, w_output, w_up, w_down.T,
             gain_attn.reshape(1, depth), gain_ffn.reshape(1, depth),
         )
-        gg = lax.dynamic_slice_in_dim(gg, index * depth, depth, 1)
+        *outs, grad_down, grad_gain_attn, grad_gain_ffn = part(total, gg, out, dx)
+        return (*outs, grad_down.T, grad_gain_attn.reshape(depth), grad_gain_ffn.reshape(depth))
     else:
         z = lax.axis_index("mp")
         segment = lax.dynamic_index_in_dim(segment_ids, z, 0, keepdims=False)

time: 207 us -> 180 us (0.87)
  Pallas kernels: 192 us -> 176 us
  local copies, waits for them, and re-layouts: 11.6 us -> 0 us
    pallas_call x1, Pallas kernels: 192 us -> 173 us  [layer(): pl.pallas_call(layer_kernel, out_shape=(jax.ShapeDtypeStruct((3, 96, D),...]
    unnamed x4 -> x0, local copies, waits for them, and re-layouts: 6.59 us -> none
    transpose x2 -> x0, local copies, waits for them, and re-layouts: 3.71 us -> none  [the longest x1 1.9 us: shards(): total[2]]
    pallas_call x0 -> x1, Pallas kernels: none -> 3.23 us  [part(): pl.pallas_call(part_kernel, out_shape=[jax.ShapeDtypeStruct(out.shape, BF...]
where the time goes in v1:
time: 180 us; the launch traced here: 177 us
  Pallas kernels  176 us (98%)
    pallas_call x1, Pallas kernels, layer(): pl.pallas_call(layer_kernel, out_shape=(jax.ShapeDtypeStruct((3, 96, D),...  173 us

profile of v1, /device:TPU:0, one launch (start us, length us, event | category | flops | bytes accessed | tf_op | source)
XLA Modules:
  0.0 177.0 jit_solution(14575295215610095660)
XLA Ops:
  0.6 173.0 %layer_with_copies.1 = (f32[3,96,768]{2,1,0:T(8,128)}, f32[8,128]{1,0:T(8,128)}, bf16[4,128,768]{2,1,0:T(8,128)(2,1)}, bf16[4,128,768]{2,1,0:T(8,128)(2,1)}, bf16[2,4,8,96,768]{4,3,2,1,0:T(8,128)(2,1)}) custom-call(bf16[4,128,768]{2,1,0:T(8,128)(2,1)} %x_in.1, bf16[4,128,768]{2,1,0:T(8,128)(2,1)} %ct_in.1, s32[4,512]{1,0:T(4,128)} %seg_ref.1, ...), custom_call_target="tpu_custom_call" | custom-call | tf_op jit(solution)/shard_map/layer_with_copies/pallas_call | solution.py:733
  173.7 3.2 %part_outputs.1 = (bf16[4,128,768]{2,1,0:T(8,128)(2,1)}, bf16[4,128,768]{2,1,0:T(8,128)(2,1)}, f32[96,192]{1,0:T(8,128)}, f32[96,192]{1,0:T(8,128)}, f32[96,192]...) custom-call(f32[3,96,768]{2,1,0:T(8,128)} %get-tuple-element.24.tota, ...), custom_call_target="tpu_custom_call" | custom-call | tf_op jit(solution)/shard_map/part_outputs/pallas_call | solution.py:801

commit v2 on v0

--- a/solution.py
+++ b/solution.py
@@ -165,6 +165,25 @@
 BLOCK = 128
 LEN = 512
 
+FIRST = ('b1','a1','z01','z02','z03','x')
+SECOND = ('p00','p10','p01','iz11','f00','p02','iz12','p03','f01','iz13','a2','oz11','f02','oz12','oz13','b2','f03')
+THIRD = ()
+ATTEND = {0: ("p11","z21","iz22"), 1: ("iz23",), 2: ("p12",), 3: ("f10",), 4: ("c","p20"), 5: ("p13",), 6: ("f11", "oz22"), 7: ("p21",), 8: ("oz23",), 9: ("f12",), 10: ("p22","f13")}
+AFTER_NORM = ("p23","f20")
+UP = {0: ("f21",), 1: ("f22",), 3: ("f23",)}
+TURN = {}
+GRAD_DOWN = {}
+AFTER_GRAD_DOWN = ()
+DOWN = {0: ("e20",), 1: ("e21",), 2: ("e22",), 3: ("e23",)}
+UP_BACK = {}
+AFTER_NORM_BACK = ()
+ATTEND_BACK = {
+    0: ("l20", "l21", "l22", "l23"), 1: ("e10", "e11"), 2: ("e12", "e13"), 5: ("l10", "l11"),
+    6: ("r2",), 7: ("l12",), 8: ("l13",), 10: ("e00", "r1"), 11: ("e01", "t2"),
+}
+AFTER_ROWS = ("e02", "e03", "t1")
+LAST = ("l00", "l01", "l02", "l03", "r0")
+
 
 def block(i):
     return pl.ds(pl.multiple_of(i * BLOCK, BLOCK), BLOCK)
@@ -180,11 +199,11 @@
 
 def layer_kernel(
     x_in, ct_in, seg_ref, wq_ref, wk_ref, wv_ref, wo_ref, wup_ref, wdown_ref, ga_ref, gf_ref,
-    total_ref, gain_ref, outs_ref, dxs_ref, wide_ref,
-    own, gain_own, gain_all, attn, held, x_ref, ct_ref, out_ref, dx_ref,
-    nrm, na_t, nf_t, ct_t, ga_t, qb, kb, vb, cb, lse_ref, bias, mid, acc, act, gp,
-    staged, sums, from_core, corner, from_plane, from_z, small, small_z, gain_sum,
-    local_sem, held_sem, zs, zr, xs, xr, ys, yr, ds, dr, cs, cr, gs, gr, as_, ar,
+    outs_ref, dxs_ref, q_ref, k_ref, v_ref, o_ref, up_ref, down_ref, gain_a_ref, gain_f_ref,
+    gain_own, gain_all, weights, x_ref, ct_ref, out_ref,
+    nrm, na_t, nf_t, ct_t, qb, kb, vb, cb, lse_ref, bias, mid, acc, act, gp,
+    staged, sums, from_core, corner, from_plane, from_z, small, small_z, gain_sum, gain_parts, gain_own_sum,
+    local_sem, zs, zr, xs, xr, ys, yr, ds, dr, cs, cr, gs, gr, as_, ar,
     ecs, ecr, eks, ekr, eps, epr, ezs, ezr, egs, egr, egzs, egzr,
 ):
     dp, z, c, nx, ny, nc = place()
@@ -196,11 +215,11 @@
     for i in range(1, 4):
         pl.semaphore_signal(barrier, inc=1, device_id=(dp, lax.rem(z + i, 4)), device_id_type=MESH)
 
-    own[0] = jnp.concatenate(
+    weights[0, z, dp] = jnp.concatenate(
         [wq_ref[...], wv_ref[...], wk_ref[...], wo_ref[...].T], axis=1
     )
-    own[1] = wup_ref[...]
-    own[2] = wdown_ref[...].T
+    weights[1, z, dp] = wup_ref[...]
+    weights[2, z, dp] = wdown_ref[...]
     gain_own[...] = jnp.zeros_like(gain_own)
     gain_own[0:1, 0:96] = ga_ref[...]
     gain_own[1:2, 0:96] = gf_ref[...]
@@ -221,62 +240,60 @@
         pltpu.make_async_copy(src.at[z], dst.at[z], local_sem.at[i]).wait()
 
     def tile(g, q, d):
-        return attn.at[q, d] if g == 0 else wide_ref.at[g - 1, q, d]
-
-    def z_copy(g, q, side):
-        to = z + (1 if side else -1)
-        src = own.at[g] if q is None else tile(g, q, dp)
-        q = z if q is None else q
-        return send(src, tile(g, q, dp), zs.at[g, q, side], zr.at[g, q], (dp, to))
-
-    def z_pass(g, q):
-        origin = z if q is None else q
-
-        @pl.when((origin <= z) & (z < 3))
-        def _():
-            z_copy(g, q, 1).start()
-
-        @pl.when((origin >= z) & (z > 0))
-        def _():
-            z_copy(g, q, 0).start()
+        return weights.at[g, q, d]
+
+    mate = z + 1 - 2 * lax.rem(z, 2)
+    far_inner = 2 - z // 2
+    outer = (z == 0) | (z == 3)
+    other_side = 2 * (1 - z // 2)
+
+    def z_copy(g, q, side, to):
+        return send(tile(g, q, dp), tile(g, q, dp), zs.at[g, q, side], zr.at[g, q], (dp, to))
+
+    def passes_on(q):
+        return jnp.logical_not(outer) & (q // 2 != z // 2)
+
+    def own_z(g):
+        z_copy(g, z, 0, mate).start()
+        z_copy(g, z, 1, far_inner).start()
 
     def z_done(g, q):
-        @pl.when((q <= z) & (z < 3))
-        def _():
-            z_copy(g, q, 1).wait_send()
-
-        @pl.when((q >= z) & (z > 0))
-        def _():
-            z_copy(g, q, 0).wait_send()
-
-    def x_copy(g, q, src=None):
-        src = tile(g, q, dp) if src is None else src
-        return send(src, tile(g, q, dp), xs.at[g, q], xr.at[g, q], (nx, z))
-
-    def y_copy(g, q, src=None):
-        src = tile(g, q, dp) if src is None else src
-        return send(src, tile(g, q, dp), ys.at[g, q], yr.at[g, q], (ny, z))
-
-    def core_copy(g, q, pos, src=None):
+        @pl.when(q == z)
+        def _():
+            z_copy(g, q, 0, mate).wait_send()
+            z_copy(g, q, 1, far_inner).wait_send()
+
+        @pl.when(passes_on(q))
+        def _():
+            z_copy(g, q, 0, mate).wait_send()
+
+    def x_copy(g, q):
+        return send(tile(g, q, dp), tile(g, q, dp), xs.at[g, q], xr.at[g, q], (nx, z))
+
+    def y_copy(g, q):
+        return send(tile(g, q, dp), tile(g, q, dp), ys.at[g, q], yr.at[g, q], (ny, z))
+
+    def core_copy(g, q, pos):
         d = 2 * pos + c
-        src = tile(g, q, d) if src is None else src
-        return send(src, tile(g, q, d), cs.at[g, q, pos], cr.at[g, q, pos], (nc, z))
+        return send(tile(g, q, d), tile(g, q, d), cs.at[g, q, pos], cr.at[g, q, pos], (nc, z))
 
     def forward(g, q, along_y):
         src, to = (nx, ny) if along_y else (ny, nx)
         return send(tile(g, q, src), tile(g, q, src), ds.at[g, q], dr.at[g, q], (to, z))
 
-    def own_start(g):
-        z_pass(g, None)
-        x_copy(g, z, own.at[g]).start()
-        y_copy(g, z, own.at[g]).start()
-        core_copy(g, z, yx, own.at[g]).start()
-        pltpu.make_async_copy(own.at[g], tile(g, z, dp), local_sem.at[4 + g]).start()
+    def own_plane(g):
+        x_copy(g, z).start()
+        y_copy(g, z).start()
+        core_copy(g, z, yx).start()
 
     def z_step(g, k):
         q = nearest(z, k)
-        send(tile(g, q, dp), tile(g, q, dp), zs.at[g, q, 0], zr.at[g, q], (dp, z)).wait_recv()
-        z_pass(g, q)
+        z_copy(g, q, 0, mate).wait_recv()
+
+        @pl.when(passes_on(q))
+        def _():
+            z_copy(g, q, 0, mate).start()
+
         x_copy(g, q).start()
         y_copy(g, q).start()
         core_copy(g, q, yx).start()
@@ -285,14 +302,14 @@
         q = nearest(z, k)
         x_copy(g, q).wait_recv()
 
-        @pl.when(q < 2)
+        @pl.when(lax.rem(q, 2) == 0)
         def _():
             forward(g, q, True).start()
 
         core_copy(g, q, yx_x).start()
         y_copy(g, q).wait_recv()
 
-        @pl.when(q >= 2)
+        @pl.when(lax.rem(q, 2) == 1)
         def _():
             forward(g, q, False).start()
 
@@ -317,11 +334,11 @@
             x_copy(g, q).wait_send()
             y_copy(g, q).wait_send()
 
-            @pl.when(q < 2)
+            @pl.when(lax.rem(q, 2) == 0)
             def _():
                 forward(g, q, True).wait_send()
 
-            @pl.when(q >= 2)
+            @pl.when(lax.rem(q, 2) == 1)
             def _():
                 forward(g, q, False).wait_send()
 
@@ -330,17 +347,11 @@
 
         loop(4, step)
 
-    def own_ready(g):
-        pltpu.make_async_copy(own.at[g], tile(g, z, dp), local_sem.at[4 + g]).wait()
-
-    def hold(g, q, slot):
-        return pltpu.make_async_copy(wide_ref.at[g - 1, q], held.at[slot], held_sem.at[slot])
-
     def out_core(g, q):
-        return send(staged.at[q], from_core.at[g, q], ecs.at[g, q], ecr.at[g, q], (nc, z))
+        return send(staged.at[q], from_core.at[g % 2, q], ecs.at[g, q], ecr.at[g, q], (nc, z))
 
     def out_corner(g, q):
-        to = nx + (ny - nx) * (q // 2)
+        to = nx + (ny - nx) * lax.rem(q, 2)
         return send(sums.at[g, q, yx_d], corner.at[g, q], eks.at[g, q], ekr.at[g, q], (to, z))
 
     def out_plane(g, q, side):
@@ -350,23 +361,14 @@
             sums.at[g, q, pos], from_plane.at[g, q, side], eps.at[g, q, side], epr.at[g, q, side], (to, z)
         )
 
-    def out_z(g, q):
-        return send(sums.at[g, q, yx], from_z.at[g, z], ezs.at[g, q], ezr.at[g, z], (dp, q))
-
-    def core_add(g, q):
-        out_core(g, q).wait_recv()
-
-        def step(pos):
-            sums[g, q, pos] = (
-                sums[g, q, pos].astype(F32) + from_core[g, q, pos].astype(F32)
-            ).astype(BF)
-
-        loop(4, step)
-        out_corner(g, q).start()
-        out_plane(g, q, q // 2).start()
+    def out_z(g, q, slot, to):
+        return send(sums.at[g, q, yx], from_z.at[g, slot], ezs.at[g, q], ezr.at[g, slot], (dp, to))
+
+    def in_z(g, slot):
+        return send(sums.at[g, 0, yx], from_z.at[g, slot], ezs.at[g, 0], ezr.at[g, slot], (dp, mate))
 
     def corner_add(g, q):
-        side = 1 - q // 2
+        side = 1 - lax.rem(q, 2)
         pos = yx_x + (yx_y - yx_x) * side
         out_corner(g, q).wait_recv()
         sums[g, q, pos] = (sums[g, q, pos].astype(F32) + corner[g, q].astype(F32)).astype(BF)
@@ -381,17 +383,36 @@
             + from_plane[g, q, 1].astype(F32)
         ).astype(BF)
 
-        @pl.when(z != q)
-        def _():
-            out_z(g, q).start()
+        @pl.when(q == mate)
+        def _():
+            out_z(g, q, 0, mate).start()
+
+        @pl.when(outer & (q // 2 != z // 2))
+        def _():
+            out_z(g, q, 2 + lax.rem(q, 2), mate).start()
+
+    def relay(g):
+        @pl.when(jnp.logical_not(outer))
+        def _():
+            for j in range(2):
+                q = other_side + j
+                in_z(g, 2 + j).wait_recv()
+                sums[g, q, yx] = (
+                    sums[g, q, yx].astype(F32) + from_z[g, 2 + j].astype(F32)
+                ).astype(BF)
+                out_z(g, q, 1, q).start()
 
     def last_add(g):
-        total = sums[g, z, yx].astype(F32)
-        for j in range(1, 4):
-            q = lax.rem(z + j, 4)
-            send(sums.at[g, q, yx], from_z.at[g, q], ezs.at[g, q], ezr.at[g, q], (dp, q)).wait_recv()
-            total = total + from_z[g, q].astype(F32)
-        total_ref[g] = total
+        in_z(g, 0).wait_recv()
+        in_z(g, 1).wait_recv()
+        total = sums[g, z, yx].astype(F32) + from_z[g, 0].astype(F32) + from_z[g, 1].astype(F32)
+        if g == 0:
+            q_ref[...] = total[:, 0:192]
+            v_ref[...] = total[:, 192:384]
+            k_ref[...] = total[:, 384:576]
+            o_ref[...] = total[:, 576:768].T
+        else:
+            (up_ref if g == 1 else down_ref)[...] = total
 
     def grads_sent(g):
         def step(q):
@@ -401,26 +422,40 @@
 
             @pl.when(z != q)
             def _():
-                out_z(g, q).wait_send()
+                out_z(g, q, 0, mate).wait_send()
 
         loop(4, step)
 
-    def emit(g, q, left, right, left_2=None, right_2=None):
+    def grad_rows(half, left, right, more):
+        v = natural(left[:, half].reshape(384, LEN), right)
+        if more is None:
+            return ((0, v),)
+        v2 = natural(more[0][:, half].reshape(384, LEN), more[1])
+        return ((0, v[:, 0:512]), (512, v[:, 512:640] + v2[:, 0:128]), (640, v2[:, 128:256]))
+
+    def emit_other(g, q, left, right, more=None):
         if g < 2:
             out_core(g + 1, q).wait_send()
-        for other in (True, False):
-            half = 1 - c if other else c
-            dst = staged.at[q] if other else sums.at[g, q]
-            v = natural(left[:, half].reshape(384, LEN), right)
-            if right_2 is None:
-                dst[...] = v.astype(BF).reshape(4, 96, D)
-            else:
-                v2 = natural(left_2[:, half].reshape(384, LEN), right_2)
-                dst[:, :, 0:512] = v[:, 0:512].astype(BF).reshape(4, 96, 512)
-                dst[:, :, 512:640] = (v[:, 512:640] + v2[:, 0:128]).astype(BF).reshape(4, 96, 128)
-                dst[:, :, 640:768] = v2[:, 128:256].astype(BF).reshape(4, 96, 128)
-            if other:
-                out_core(g, q).start()
+        for first, v in grad_rows(1 - c, left, right, more):
+            staged[q, :, :, first : first + v.shape[1]] = v.astype(BF).reshape(4, 96, v.shape[1])
+        out_core(g, q).start()
+
+    def emit_own(g, q, left, right, more=None):
+        pieces = grad_rows(c, left, right, more)
+        out_core(g, q).wait_recv()
+        for first, v in pieces:
+            lanes = slice(first, first + v.shape[1])
+            theirs = from_core[g % 2, q, :, :, lanes].astype(F32)
+            sums[g, q, :, :, lanes] = (v.reshape(4, 96, v.shape[1]) + theirs).astype(BF)
+        out_corner(g, q).start()
+
+        @pl.when(q >= 1)
+        def _():
+            out_plane(g, q - 1, lax.rem(q - 1, 2)).start()
+
+        @pl.when(q == 3)
+        def _():
+            out_plane(g, q, lax.rem(q, 2)).start()
 
     def put_t(dst, i, v):
         dst[:, :, :, block(i)] = v.T.reshape(4, 2, 96, BLOCK)
@@ -434,27 +469,43 @@
         def _():
             acc[...] += value
 
-    own_start(0)
+    steps = {
+        "a": own_z, "b": own_plane, "z": z_step, "p": plane_step, "f": far_step,
+        "x": lambda: rows_start(0, x_in, x_ref), "c": lambda: rows_start(1, ct_in, ct_ref),
+        "e": corner_add, "l": plane_add, "r": relay, "t": last_add,
+    }
+
+    def take(names):
+        for name in names:
+            act_on = functools.partial(steps[name.lstrip("io")[0]], *map(int, name.lstrip("io")[1:]))
+            if name[0] in "io":
+                pl.when(outer if name[0] == "o" else jnp.logical_not(outer))(act_on)
+            else:
+                act_on()
+
+    def serve(now, table):
+        for due, names in table.items():
+            pl.when(now == due)(functools.partial(take, names))
+
+    own_z(0)
+    own_plane(0)
     for i in range(1, 8):
         to = lax.rem(dp + i, 8)
         send(gain_own, gain_all.at[dp], gs.at[to], gr.at[dp], (to, z)).start()
     gain_all[dp] = gain_own[...]
-    loop(3, lambda k: z_step(0, k + 1))
-    rows_start(0, x_in, x_ref)
-    own_start(1)
+    take(FIRST)
     seg_row = seg_ref[pl.ds(z, 1)].astype(F32)
     seg_col = jnp.broadcast_to(seg_row, (8, LEN)).T[:, 0:1]
     bias[...] = jnp.where(seg_col == seg_row, 0.0, -1e30)
     gain_sum[...] = jnp.zeros_like(gain_sum)
-    loop(4, lambda k: plane_step(0, k))
-    loop(3, lambda k: z_step(1, k + 1))
-    own_start(2)
+    gain_parts[...] = jnp.zeros_like(gain_parts)
+    take(SECOND)
     for i in range(1, 8):
         other = lax.rem(dp + i, 8)
         send(gain_own, gain_all.at[other], gs.at[other], gr.at[other], (other, z)).wait_recv()
     gain_a = gain_row(gain_all, 0)
     gain_f = gain_row(gain_all, 1)
-    loop(4, lambda k: far_step(0, k))
+    take(THIRD)
     rows_wait(0, x_in, x_ref)
 
     def norm_a(i):
@@ -464,12 +515,11 @@
         put_t(na_t, i, normed)
 
     loop(4, norm_a)
-    own_ready(0)
 
     def attend(i):
         q = nearest(z, i)
         core_ready(0, q)
-        w = attn[q].reshape(D, D)
+        w = weights[0, q].reshape(D, D)
         p = natural(nrm[...], w[:, 0:640])
         q8 = p[:, 0:256].astype(BF) * jnp.asarray(0.125, BF)
         v = p[:, 128:384].astype(BF)
@@ -492,22 +542,14 @@
                     cb[q, rs] += part
                 lane = lax.broadcasted_iota(jnp.int32, (256, 128), 1)
                 lse_ref[rs] = jnp.where(lane == 3 * q + h, m + jnp.log(total), lse_ref[rs])
-            if h == 0:
-                plane_step(1, i)
-            if h == 1:
-                @pl.when(i < 3)
-                def _():
-                    z_step(2, i + 1)
+            serve(3 * i + h, ATTEND)
 
     loop(4, attend)
-    rows_start(1, ct_in, ct_ref)
 
     def attend_out(i):
-        add(i, against(cb[i], attn[i].reshape(D, D)[:, 512:768]))
-        far_step(1, i)
+        add(i, against(cb[i], weights[0, i].reshape(D, D)[:, 512:768]))
 
     loop(4, attend_out)
-    own_ready(1)
 
     def norm_f(i):
         m = x_ref[i].astype(F32) + acc[block(i)]
@@ -518,91 +560,61 @@
         put_t(nf_t, i, normed)
 
     loop(4, norm_f)
-    q = nearest(z, 0)
-    core_ready(1, q)
-    hold(1, q, 0).start()
-
+    take(AFTER_NORM)
     def up(i):
         q = nearest(z, i)
-        slot = lax.rem(i, 2)
-
-        @pl.when(i < 3)
-        def _():
-            later = nearest(z, i + 1)
-            core_ready(1, later)
-            hold(1, later, 1 - slot).start()
-
-        hold(1, q, slot).wait()
-        w = held[slot].reshape(D, D)
+        core_ready(1, q)
+        w = weights[1, q].reshape(D, D)
         for r in range(2):
             rs = slice(256 * r, 256 * (r + 1))
             h = natural(nrm[rs], w)
             cdf = 0.5 + 0.5 * lax.erf(h * 0.7071067811865476)
             act[q, rs] = (h * cdf).astype(BF)
             gp[q, rs] = (cdf + h * (jnp.exp(-0.5 * h * h) * 0.3989422804014327)).astype(BF)
-        plane_step(2, i)
+        serve(i, UP)
 
     loop(4, up)
     rows_wait(1, ct_in, ct_ref)
 
     def turn_ct(i):
         put_t(ct_t, i, ct_ref[i])
-        far_step(2, i)
+        serve(i, TURN)
 
     loop(4, turn_ct)
-    own_ready(2)
 
     def grad_down(i):
-        emit(2, i, ct_t, act[i])
+        emit_other(2, i, ct_t, act[i])
 
         @pl.when(i > 0)
         def _():
-            core_add(2, i - 1)
+            emit_own(2, i - 1, ct_t, act[i - 1])
+
+        serve(i, GRAD_DOWN)
 
     loop(4, grad_down)
-    core_add(2, 3)
-    q = nearest(z, 0)
-    core_ready(2, q)
-    hold(2, q, 0).start()
+    emit_own(2, 3, ct_t, act[3])
+    take(AFTER_GRAD_DOWN)
 
     def down(i):
         q = nearest(z, i)
-        slot = lax.rem(i, 2)
-
-        @pl.when(i < 3)
-        def _():
-            later = nearest(z, i + 1)
-            core_ready(2, later)
-            hold(2, later, 1 - slot).start()
-
-        hold(2, q, slot).wait()
-        w = held[slot].reshape(D, D)
+        core_ready(2, q)
+        w = weights[2, q].reshape(D, D)
         gp[q] = (natural(ct_ref[...].reshape(LEN, D), w) * gp[q].astype(F32)).astype(BF)
         add(i, against(act[q], w))
+        serve(i, DOWN)
 
     loop(4, down)
-    hold(1, 0, 0).start()
     out_ref[...] = (mid[...] + acc[...]).astype(BF).reshape(4, BLOCK, D)
     rows_start(2, out_ref, outs_ref)
-    loop(4, lambda k: corner_add(2, k))
 
     def up_back(i):
-        slot = lax.rem(i, 2)
-
-        @pl.when(i < 3)
-        def _():
-            hold(1, i + 1, 1 - slot).start()
-
-        hold(1, i, slot).wait()
-        add(i, against(gp[i], held[slot].reshape(D, D)))
-        emit(1, i, nf_t, gp[i])
-
-        @pl.when(i > 0)
-        def _():
-            core_add(1, i - 1)
+        emit_other(1, i, nf_t, gp[i])
+        add(i, against(gp[i], weights[1, i].reshape(D, D)))
+        emit_own(1, i, nf_t, gp[i])
+
+        serve(i, UP_BACK)
 
     loop(4, up_back)
-    core_add(1, 3)
 
     def norm_f_back(i):
         xhat, scale = norm(mid[block(i)])
@@ -612,12 +624,13 @@
         mid[block(i)] = grad_middle
         attended = grad_middle.astype(BF)
         nrm[block(i)] = attended
-        put_t(ga_t, i, attended)
+        put_t(ct_t, i, attended)
 
     loop(4, norm_f_back)
+    take(AFTER_NORM_BACK)
 
     def attend_back(i):
-        w = attn[i].reshape(D, D)
+        w = weights[0, i].reshape(D, D)
         dctx = between(natural(nrm[...], w[:, 512:768]), 64, 192).astype(BF)
         q8, v, k, cx = qb[i], vb[i], kb[i], cb[i]
         dq = jnp.zeros((LEN, 256), F32)
@@ -633,72 +646,83 @@
             dq += between(natural(ds_, k), 64 * h, 64)
             dk += between(inner(ds_, q8), 64 * h, 64)
             dv += between(inner(p.astype(BF), dctx), 64 + 64 * h, 64)
-            if h == 0:
-                plane_add(2, i)
-            if h == 1:
-                corner_add(1, i)
+            serve(3 * i + h, ATTEND_BACK)
         dq = dq * 0.125
         d = jnp.concatenate(
             [dq[:, 0:128], dq[:, 128:256] + dv[:, 0:128], dv[:, 128:256], dk], axis=1
         ).astype(BF)
+
+        @pl.when(i < 3)
+        def _():
+            emit_other(0, i, na_t, d, (ct_t, cx))
+
         add(i, against(d, w[:, 0:640]))
-        emit(0, i, na_t, d, ga_t, cx)
-
-        @pl.when(i > 0)
-        def _():
-            core_add(0, i - 1)
+
+        @pl.when(i < 3)
+        def _():
+            emit_own(0, i, na_t, d, (ct_t, cx))
+
+        @pl.when(i == 3)
+        def _():
+            nrm[:, 0:640] = d
 
     loop(4, attend_back)
-    core_add(0, 3)
 
     def norm_a_back(i):
         xhat, scale = norm(x_ref[i].astype(F32))
         back, grad_gain = norm_back(acc[block(i)], xhat, scale, gain_a)
         gain_sum[0:1] += grad_gain[None]
-        dx_ref[i] = (mid[block(i)] + back).astype(BF)
+        ct_ref[i] = (mid[block(i)] + back).astype(BF)
 
     loop(4, norm_a_back)
-    rows_start(3, dx_ref, dxs_ref)
-    last_add(2)
+    rows_start(3, ct_ref, dxs_ref)
+    emit_other(0, 3, na_t, nrm[:, 0:640], (ct_t, cb[3]))
+    for i in range(2):
+        for p in range(8):
+            gain_parts[p, i : i + 1, 0:96] = gain_sum[i : i + 1, 96 * p : 96 * (p + 1)]
 
     def small_copy(i):
-        return send(gain_sum, small.at[i], egs.at[i], egr.at[i], ((nc, nx, ny)[i], z))
-
-    def small_add(i):
-        small_copy(i).wait()
-        gain_sum[...] += small[i]
-
-    small_copy(0).start()
-    loop(4, lambda k: corner_add(0, k))
-    small_add(0)
-    small_copy(1).start()
-    loop(4, lambda k: plane_add(1, k))
-    small_add(1)
-    small_copy(2).start()
-    last_add(1)
-    small_add(2)
+        to = lax.rem(dp + i, 8)
+        return send(gain_parts.at[to], small.at[dp], egs.at[to], egr.at[dp], (to, z))
+
+    def small_in(i):
+        other = lax.rem(dp + i, 8)
+        return send(gain_parts.at[other], small.at[other], egs.at[other], egr.at[other], (other, z))
+
+    for i in range(1, 8):
+        small_copy(i).start()
+    emit_own(0, 3, na_t, nrm[:, 0:640], (ct_t, cb[3]))
+    take(AFTER_ROWS)
+    total = gain_parts[dp]
+    for i in range(1, 8):
+        small_in(i).wait_recv()
+        total = total + small[lax.rem(dp + i, 8)]
+    gain_own_sum[...] = total
     for j in range(1, 4):
         q = lax.rem(z + j, 4)
-        send(gain_sum, small_z.at[z], egzs.at[q], egzr.at[z], (dp, q)).start()
-    loop(4, lambda k: plane_add(0, k))
-    total = gain_sum[...]
-    for j in range(1, 4):
-        q = lax.rem(z + j, 4)
-        cp = send(gain_sum, small_z.at[q], egzs.at[q], egzr.at[q], (dp, q))
-        cp.wait()
-        total = total + small_z[q]
-    gain_ref[...] = total
-    last_add(0)
-
+        send(gain_own_sum, small_z.at[z], egzs.at[q], egzr.at[z], (dp, q)).start()
+    take(LAST)
     for i in range(1, 8):
         other = lax.rem(dp + i, 8)
         send(gain_own, gain_all.at[other], gs.at[other], gr.at[other], (other, z)).wait_send()
+        small_copy(i).wait_send()
     for g in range(3):
         weights_sent(g)
-        grads_sent(g)
+    grads_sent(2)
+    grads_sent(1)
     loop(4, lambda q: out_core(0, q).wait_send())
     rows_wait(2, out_ref, outs_ref)
-    rows_wait(3, dx_ref, dxs_ref)
+    total = gain_own_sum[...]
+    for j in range(1, 4):
+        q = lax.rem(z + j, 4)
+        cp = send(gain_own_sum, small_z.at[q], egzs.at[q], egzr.at[q], (dp, q))
+        cp.wait()
+        total = total + small_z[q]
+    gain_a_ref[...] = total[0:1, 0:96]
+    gain_f_ref[...] = total[1:2, 0:96]
+    rows_wait(3, ct_ref, dxs_ref)
+    last_add(0)
+    grads_sent(0)
 
 
 def layer(x, ct, segment_ids, w_query, w_key, w_value, w_output, w_up, w_down, gain_attn, gain_ffn):
@@ -709,27 +733,25 @@
     return pl.pallas_call(
         layer_kernel,
         out_shape=(
-            jax.ShapeDtypeStruct((3, 96, D), F32),
-            jax.ShapeDtypeStruct((8, D), F32),
             jax.ShapeDtypeStruct(x.shape, BF),
             jax.ShapeDtypeStruct(x.shape, BF),
-            jax.ShapeDtypeStruct((2, 4, 8, 96, D), BF),
+            *(jax.ShapeDtypeStruct(n, F32) for n in [(96, 192)] * 3 + [(192, 96)] + [(96, D)] * 2 + [(1, 96)] * 2),
         ),
         in_specs=[anywhere] * 2 + [vmem] * 9,
-        out_specs=(vmem, vmem, anywhere, anywhere, anywhere),
+        out_specs=[anywhere] * 2 + [vmem] * 8,
         scratch_shapes=[
-            vm((3, 96, D), BF), vm((16, 128), BF), vm((8, 16, 128), BF),
-            vm((4, 8, 96, D), BF), vm((2, 8, 96, D), BF),
-            vm((4, BLOCK, D), BF), vm((4, BLOCK, D), BF), vm((4, BLOCK, D), BF), vm((4, BLOCK, D), BF),
+            vm((16, 128), BF), vm((8, 16, 128), BF),
+            vm((3, 4, 8, 96, D), BF),
+            vm((4, BLOCK, D), BF), vm((4, BLOCK, D), BF), vm((4, BLOCK, D), BF),
             vm((LEN, D), BF),
-            vm((4, 2, 96, LEN), BF), vm((4, 2, 96, LEN), BF), vm((4, 2, 96, LEN), BF), vm((4, 2, 96, LEN), BF),
+            vm((4, 2, 96, LEN), BF), vm((4, 2, 96, LEN), BF), vm((4, 2, 96, LEN), BF),
             vm((4, LEN, 256), BF), vm((4, LEN, 256), BF), vm((4, LEN, 256), BF), vm((4, LEN, 256), BF),
             vm((LEN, 128), F32), vm((LEN, LEN), F32), vm((LEN, D), F32), vm((LEN, D), F32),
             vm((4, LEN, D), BF), vm((4, LEN, D), BF),
-            vm((4, 4, 96, D), BF), vm((3, 4, 4, 96, D), BF), vm((3, 4, 4, 96, D), BF),
+            vm((4, 4, 96, D), BF), vm((3, 4, 4, 96, D), BF), vm((2, 4, 4, 96, D), BF),
             vm((3, 4, 96, D), BF), vm((3, 4, 2, 96, D), BF), vm((3, 4, 96, D), BF),
-            vm((3, 8, D), F32), vm((4, 8, D), F32), vm((8, D), F32),
-            sem((7,)), sem((2,)),
+            vm((8, 8, 128), F32), vm((4, 8, 128), F32), vm((8, D), F32), vm((8, 8, 128), F32), vm((8, 128), F32),
+            sem((4,)),
             sem((3, 4, 2)), sem((3, 4)),
             sem((3, 4)), sem((3, 4)),
             sem((3, 4)), sem((3, 4)),
@@ -741,7 +763,7 @@
             sem((3, 4)), sem((3, 4)),
             sem((3, 4, 2)), sem((3, 4, 2)),
             sem((3, 4)), sem((3, 4)),
-            sem((3,)), sem((3,)),
+            sem((8,)), sem((8,)),
             sem((4,)), sem((4,)),
         ],
         compiler_params=pltpu.CompilerParams(
@@ -754,18 +776,47 @@
 VMEM_LIMIT = 62 * 2**20
 
 
+def part_kernel(*refs):
+    count = (len(refs) - 2) // 3
+    sources, targets, held, (arrive, leave) = (
+        refs[:count], refs[count : 2 * count], refs[2 * count : 3 * count], refs[3 * count :]
+    )
+    coming = [pltpu.make_async_copy(sources[i], held[i], arrive.at[i]) for i in range(count)]
+    going = [pltpu.make_async_copy(held[i], targets[i], leave.at[i]) for i in range(count)]
+    for copy in coming:
+        copy.start()
+    for copy_in, copy_out in zip(coming, going):
+        copy_in.wait()
+        copy_out.start()
+    for copy in going:
+        copy.wait()
+
+
+def part(*results):
+    anywhere = pl.BlockSpec(memory_space=pl.ANY)
+    return pl.pallas_call(
+        part_kernel,
+        out_shape=[jax.ShapeDtypeStruct(r.shape, r.dtype) for r in results],
+        in_specs=[anywhere] * len(results),
+        out_specs=[anywhere] * len(results),
+        scratch_shapes=[pltpu.VMEM(r.shape, r.dtype) for r in results]
+        + [pltpu.SemaphoreType.DMA((len(results),))] * 2,
+        name="part_outputs",
+    )(*results)
+
+
 def shards(
     inputs, segment_ids, w_query, w_key, w_value, w_output, w_up, w_down, gain_attn, gain_ffn, cotangent,
     *, parts, quarters,
 ):
     depth, width = w_query.shape
-    index = lax.axis_index("dp")
     if parts == 8 and quarters == 4:
-        total, gg, out, dx, _ = layer(
-            inputs, cotangent, segment_ids, w_query, w_key, w_value, w_output, w_up, w_down,
+        results = layer(
+            inputs, cotangent, segment_ids, w_query, w_key, w_value, w_output, w_up, w_down.T,
             gain_attn.reshape(1, depth), gain_ffn.reshape(1, depth),
         )
-        gg = lax.dynamic_slice_in_dim(gg, index * depth, depth, 1)
+        *outs, grad_down, grad_gain_attn, grad_gain_ffn = part(*results)
+        return (*outs, grad_down.T, grad_gain_attn.reshape(depth), grad_gain_ffn.reshape(depth))
     else:
         z = lax.axis_index("mp")
         segment = lax.dynamic_index_in_dim(segment_ids, z, 0, keepdims=False)

time: 207 us -> 165 us (0.80)
  Pallas kernels: 192 us -> 162 us
  local copies, waits for them, and re-layouts: 11.6 us -> 0 us
    pallas_call x1 -> x2, Pallas kernels: 192 us -> 162 us  [the longest x1 159 us: layer(): pl.pallas_call(layer_kernel, out_shape=(jax.ShapeDtypeStruct(x.shape, BF)...]
    unnamed x4 -> x0, local copies, waits for them, and re-layouts: 6.59 us -> none
    transpose x2 -> x0, local copies, waits for them, and re-layouts: 3.71 us -> none  [the longest x1 1.9 us: shards(): total[2]]
where the time goes in v2:
time: 165 us; the launch traced here: 163 us
  Pallas kernels  162 us (98%)
    pallas_call x1, Pallas kernels, layer(): pl.pallas_call(layer_kernel, out_shape=(jax.ShapeDtypeStruct(x.shape, BF)...  159 us

profile of v2, /device:TPU:0, one launch (start us, length us, event | category | flops | bytes accessed | tf_op | source)
XLA Modules:
  0.0 163.0 jit_solution(8198412758386982201)
XLA Ops:
  0.6 159.4 %layer_with_copies.1 = (bf16[4,128,768]{2,1,0:T(8,128)(2,1)}, bf16[4,128,768]{2,1,0:T(8,128)(2,1)}, f32[96,192]{1,0:T(8,128)}, f32[96,192]{1,0:T(8,128)}, f32[96...) custom-call(bf16[4,128,768]{2,1,0:T(8,128)(2,1)} %x_in.1, ...), custom_call_target="tpu_custom_call" | custom-call | tf_op jit(solution)/shard_map/layer_with_copies/pallas_call | solution.py:733
  160.0 2.8 %part_outputs.1 = (bf16[4,128,768]{2,1,0:T(8,128)(2,1)}, bf16[4,128,768]{2,1,0:T(8,128)(2,1)}, f32[96,192]{1,0:T(8,128)}, f32[96,192]{1,0:T(8,128)}, f32[96,192]...) custom-call(bf16[4,128,768]{2,1,0:T(8,128)(2,1)} %get-tuple-element., ...), custom_call_target="tpu_custom_call" | custom-call | tf_op jit(solution)/shard_map/part_outputs/pallas_call | solution.py:797

commit v3 on v2

--- a/solution.py
+++ b/solution.py
@@ -165,24 +165,29 @@
 BLOCK = 128
 LEN = 512
 
-FIRST = ('b1','a1','z01','z02','z03','x')
-SECOND = ('p00','p10','p01','iz11','f00','p02','iz12','p03','f01','iz13','a2','oz11','f02','oz12','oz13','b2','f03')
+FIRST = ("b1", "a1", "z01", "s01", "z02", "s02", "z03", "s03", "x")
+SECOND = (
+    "p00", "p10", "p01", "iz11", "is11", "f00", "p02", "iz12", "is12", "p03", "f01", "iz13", "is13", "a2",
+    "oz11", "os11", "f02", "oz12", "os12", "oz13", "os13", "b2", "f03",
+)
 THIRD = ()
-ATTEND = {0: ("p11","z21","iz22"), 1: ("iz23",), 2: ("p12",), 3: ("f10",), 4: ("c","p20"), 5: ("p13",), 6: ("f11", "oz22"), 7: ("p21",), 8: ("oz23",), 9: ("f12",), 10: ("p22","f13")}
-AFTER_NORM = ("p23","f20")
+ATTEND = {
+    0: ("p11", "z21", "s21", "iz22", "is22", "iz23", "is23"), 1: ("p12", "f10"), 2: ("c", "p20"),
+    3: ("p13",), 4: ("f11", "oz22", "os22"), 5: ("p21", "oz23", "os23"), 6: ("f12",), 7: ("p22", "f13"),
+}
+AFTER_NORM = ("p23", "f20")
+TURN = {}
 UP = {0: ("f21",), 1: ("f22",), 3: ("f23",)}
-TURN = {}
-GRAD_DOWN = {}
 AFTER_GRAD_DOWN = ()
 DOWN = {0: ("e20",), 1: ("e21",), 2: ("e22",), 3: ("e23",)}
 UP_BACK = {}
-AFTER_NORM_BACK = ()
+AFTER_NORM_BACK = ("l20", "l21", "l22", "l23")
 ATTEND_BACK = {
-    0: ("l20", "l21", "l22", "l23"), 1: ("e10", "e11"), 2: ("e12", "e13"), 5: ("l10", "l11"),
-    6: ("r2",), 7: ("l12",), 8: ("l13",), 10: ("e00", "r1"), 11: ("e01", "t2"),
+    0: ("e10", "e11"), 1: ("e12", "e13", "r20", "r21"), 3: ("l10", "l11"), 5: ("l12", "l13", "r10", "r11", "e00"),
+    7: ("t2", "e01"),
 }
 AFTER_ROWS = ("e02", "e03", "t1")
-LAST = ("l00", "l01", "l02", "l03", "r0")
+LAST = ("l00", "l01", "l02", "r00", "r01", "l03")
 
 
 def block(i):
@@ -294,6 +299,8 @@
         def _():
             z_copy(g, q, 0, mate).start()
 
+    def spread_step(g, k):
+        q = nearest(z, k)
         x_copy(g, q).start()
         y_copy(g, q).start()
         core_copy(g, q, yx).start()
@@ -348,7 +355,7 @@
         loop(4, step)
 
     def out_core(g, q):
-        return send(staged.at[q], from_core.at[g % 2, q], ecs.at[g, q], ecr.at[g, q], (nc, z))
+        return send(staged.at[q], from_core.at[q], ecs.at[g, q], ecr.at[g, q], (nc, z))
 
     def out_corner(g, q):
         to = nx + (ny - nx) * lax.rem(q, 2)
@@ -391,16 +398,15 @@
         def _():
             out_z(g, q, 2 + lax.rem(q, 2), mate).start()
 
-    def relay(g):
+    def relay(g, k):
+        q = quarter(k)
+
         @pl.when(jnp.logical_not(outer))
         def _():
-            for j in range(2):
-                q = other_side + j
-                in_z(g, 2 + j).wait_recv()
-                sums[g, q, yx] = (
-                    sums[g, q, yx].astype(F32) + from_z[g, 2 + j].astype(F32)
-                ).astype(BF)
-                out_z(g, q, 1, q).start()
+            slot = 2 + lax.rem(q, 2)
+            in_z(g, slot).wait_recv()
+            sums[g, q, yx] = (sums[g, q, yx].astype(F32) + from_z[g, slot].astype(F32)).astype(BF)
+            out_z(g, q, 1, q).start()
 
     def last_add(g):
         in_z(g, 0).wait_recv()
@@ -426,6 +432,9 @@
 
         loop(4, step)
 
+    def quarter(k):
+        return nearest(z, 3 - k)
+
     def grad_rows(half, left, right, more):
         v = natural(left[:, half].reshape(384, LEN), right)
         if more is None:
@@ -440,20 +449,22 @@
             staged[q, :, :, first : first + v.shape[1]] = v.astype(BF).reshape(4, 96, v.shape[1])
         out_core(g, q).start()
 
-    def emit_own(g, q, left, right, more=None):
+    def emit_own(g, k, left, right, more=None):
+        q = quarter(k)
         pieces = grad_rows(c, left, right, more)
         out_core(g, q).wait_recv()
         for first, v in pieces:
             lanes = slice(first, first + v.shape[1])
-            theirs = from_core[g % 2, q, :, :, lanes].astype(F32)
+            theirs = from_core[q, :, :, lanes].astype(F32)
             sums[g, q, :, :, lanes] = (v.reshape(4, 96, v.shape[1]) + theirs).astype(BF)
         out_corner(g, q).start()
 
-        @pl.when(q >= 1)
-        def _():
-            out_plane(g, q - 1, lax.rem(q - 1, 2)).start()
-
-        @pl.when(q == 3)
+        @pl.when(k >= 1)
+        def _():
+            before = quarter(k - 1)
+            out_plane(g, before, lax.rem(before, 2)).start()
+
+        @pl.when(k == 3)
         def _():
             out_plane(g, q, lax.rem(q, 2)).start()
 
@@ -470,9 +481,9 @@
             acc[...] += value
 
     steps = {
-        "a": own_z, "b": own_plane, "z": z_step, "p": plane_step, "f": far_step,
+        "a": own_z, "b": own_plane, "z": z_step, "s": spread_step, "p": plane_step, "f": far_step,
         "x": lambda: rows_start(0, x_in, x_ref), "c": lambda: rows_start(1, ct_in, ct_ref),
-        "e": corner_add, "l": plane_add, "r": relay, "t": last_add,
+        "e": lambda g, k: corner_add(g, quarter(k)), "l": lambda g, k: plane_add(g, quarter(k)), "r": relay, "t": last_add,
     }
 
     def take(names):
@@ -527,22 +538,21 @@
         qb[q] = q8
         vb[q] = v
         kb[q] = k
-        for h in range(3):
-            for r in range(2):
-                rs = slice(256 * r, 256 * (r + 1))
+        for r in range(2):
+            rs = slice(256 * r, 256 * (r + 1))
+            ctx = jnp.zeros((256, 256), F32)
+            lane = lax.broadcasted_iota(jnp.int32, (256, 128), 1)
+            lse = lse_ref[rs]
+            for h in range(3):
                 s = against(between(q8[rs], 64 * h, 64), k) + bias[rs]
                 m = jnp.max(s, axis=1, keepdims=True)
                 e = jnp.exp(s - m)
                 total = jnp.sum(e, axis=1, keepdims=True)
-                probs = (e * (1.0 / total)).astype(BF)
-                part = between(natural(probs, v), 64 + 64 * h, 64).astype(BF)
-                if h == 0:
-                    cb[q, rs] = part
-                else:
-                    cb[q, rs] += part
-                lane = lax.broadcasted_iota(jnp.int32, (256, 128), 1)
-                lse_ref[rs] = jnp.where(lane == 3 * q + h, m + jnp.log(total), lse_ref[rs])
-            serve(3 * i + h, ATTEND)
+                ctx += natural(e.astype(BF), between(v, 64 + 64 * h, 64)) * (1.0 / total)
+                lse = jnp.where(lane == 3 * q + h, m + jnp.log(total), lse)
+            lse_ref[rs] = lse
+            cb[q, rs] = ctx.astype(BF)
+            serve(2 * i + r, ATTEND)
 
     loop(4, attend)
 
@@ -561,8 +571,16 @@
 
     loop(4, norm_f)
     take(AFTER_NORM)
+    rows_wait(1, ct_in, ct_ref)
+
+    def turn_ct(i):
+        put_t(ct_t, i, ct_ref[i])
+        serve(i, TURN)
+
+    loop(4, turn_ct)
+
     def up(i):
-        q = nearest(z, i)
+        q = quarter(i)
         core_ready(1, q)
         w = weights[1, q].reshape(D, D)
         for r in range(2):
@@ -571,28 +589,16 @@
             cdf = 0.5 + 0.5 * lax.erf(h * 0.7071067811865476)
             act[q, rs] = (h * cdf).astype(BF)
             gp[q, rs] = (cdf + h * (jnp.exp(-0.5 * h * h) * 0.3989422804014327)).astype(BF)
+        emit_other(2, q, ct_t, act[q])
+
+        @pl.when(i > 0)
+        def _():
+            emit_own(2, i - 1, ct_t, act[quarter(i - 1)])
+
         serve(i, UP)
 
     loop(4, up)
-    rows_wait(1, ct_in, ct_ref)
-
-    def turn_ct(i):
-        put_t(ct_t, i, ct_ref[i])
-        serve(i, TURN)
-
-    loop(4, turn_ct)
-
-    def grad_down(i):
-        emit_other(2, i, ct_t, act[i])
-
-        @pl.when(i > 0)
-        def _():
-            emit_own(2, i - 1, ct_t, act[i - 1])
-
-        serve(i, GRAD_DOWN)
-
-    loop(4, grad_down)
-    emit_own(2, 3, ct_t, act[3])
+    emit_own(2, 3, ct_t, act[quarter(3)])
     take(AFTER_GRAD_DOWN)
 
     def down(i):
@@ -608,9 +614,10 @@
     rows_start(2, out_ref, outs_ref)
 
     def up_back(i):
-        emit_other(1, i, nf_t, gp[i])
-        add(i, against(gp[i], weights[1, i].reshape(D, D)))
-        emit_own(1, i, nf_t, gp[i])
+        q = quarter(i)
+        emit_other(1, q, nf_t, gp[q])
+        add(i, against(gp[q], weights[1, q].reshape(D, D)))
+        emit_own(1, i, nf_t, gp[q])
 
         serve(i, UP_BACK)
 
@@ -630,15 +637,16 @@
     take(AFTER_NORM_BACK)
 
     def attend_back(i):
-        w = weights[0, i].reshape(D, D)
+        q = quarter(i)
+        w = weights[0, q].reshape(D, D)
         dctx = between(natural(nrm[...], w[:, 512:768]), 64, 192).astype(BF)
-        q8, v, k, cx = qb[i], vb[i], kb[i], cb[i]
+        q8, v, k, cx = qb[q], vb[q], kb[q], cb[q]
         dq = jnp.zeros((LEN, 256), F32)
         dk = jnp.zeros((LEN, 256), F32)
         dv = jnp.zeros((LEN, 256), F32)
         for h in range(3):
             lane = lax.broadcasted_iota(jnp.int32, (LEN, 128), 1)
-            lse = jnp.sum(jnp.where(lane == 3 * i + h, lse_ref[...], 0.0), axis=1, keepdims=True)
+            lse = jnp.sum(jnp.where(lane == 3 * q + h, lse_ref[...], 0.0), axis=1, keepdims=True)
             p = jnp.exp(against(between(q8, 64 * h, 64), k) + bias[...] - lse)
             dm = between(dctx, 64 + 64 * h, 64)
             delta = jnp.sum(dm.astype(F32) * cx.astype(F32), axis=1, keepdims=True)
@@ -646,25 +654,16 @@
             dq += between(natural(ds_, k), 64 * h, 64)
             dk += between(inner(ds_, q8), 64 * h, 64)
             dv += between(inner(p.astype(BF), dctx), 64 + 64 * h, 64)
-            serve(3 * i + h, ATTEND_BACK)
         dq = dq * 0.125
         d = jnp.concatenate(
             [dq[:, 0:128], dq[:, 128:256] + dv[:, 0:128], dv[:, 128:256], dk], axis=1
         ).astype(BF)
 
-        @pl.when(i < 3)
-        def _():
-            emit_other(0, i, na_t, d, (ct_t, cx))
-
+        serve(2 * i, ATTEND_BACK)
+        emit_other(0, q, na_t, d, (ct_t, cx))
         add(i, against(d, w[:, 0:640]))
-
-        @pl.when(i < 3)
-        def _():
-            emit_own(0, i, na_t, d, (ct_t, cx))
-
-        @pl.when(i == 3)
-        def _():
-            nrm[:, 0:640] = d
+        emit_own(0, i, na_t, d, (ct_t, cx))
+        serve(2 * i + 1, ATTEND_BACK)
 
     loop(4, attend_back)
 
@@ -676,7 +675,6 @@
 
     loop(4, norm_a_back)
     rows_start(3, ct_ref, dxs_ref)
-    emit_other(0, 3, na_t, nrm[:, 0:640], (ct_t, cb[3]))
     for i in range(2):
         for p in range(8):
             gain_parts[p, i : i + 1, 0:96] = gain_sum[i : i + 1, 96 * p : 96 * (p + 1)]
@@ -691,7 +689,6 @@
 
     for i in range(1, 8):
         small_copy(i).start()
-    emit_own(0, 3, na_t, nrm[:, 0:640], (ct_t, cb[3]))
     take(AFTER_ROWS)
     total = gain_parts[dp]
     for i in range(1, 8):
@@ -748,7 +745,7 @@
             vm((4, LEN, 256), BF), vm((4, LEN, 256), BF), vm((4, LEN, 256), BF), vm((4, LEN, 256), BF),
             vm((LEN, 128), F32), vm((LEN, LEN), F32), vm((LEN, D), F32), vm((LEN, D), F32),
             vm((4, LEN, D), BF), vm((4, LEN, D), BF),
-            vm((4, 4, 96, D), BF), vm((3, 4, 4, 96, D), BF), vm((2, 4, 4, 96, D), BF),
+            vm((4, 4, 96, D), BF), vm((3, 4, 4, 96, D), BF), vm((4, 4, 96, D), BF),
             vm((3, 4, 96, D), BF), vm((3, 4, 2, 96, D), BF), vm((3, 4, 96, D), BF),
             vm((8, 8, 128), F32), vm((4, 8, 128), F32), vm((8, D), F32), vm((8, 8, 128), F32), vm((8, 128), F32),
             sem((4,)),

time: 165 us -> 160 us (0.970)
  Pallas kernels: 162 us -> 158 us
    pallas_call x1, Pallas kernels: 159 us -> 155 us  [layer(): pl.pallas_call(layer_kernel, out_shape=(jax.ShapeDtypeStruct(x.shape, BF)...]
where the time goes in v3:
time: 160 us; the launch traced here: 159 us
  Pallas kernels  158 us (99%)
    pallas_call x1, Pallas kernels, layer(): pl.pallas_call(layer_kernel, out_shape=(jax.ShapeDtypeStruct(x.shape, BF)...  155 us

profile of v3, /device:TPU:0, one launch (start us, length us, event | category | flops | bytes accessed | tf_op | source)
XLA Modules:
  0.0 158.9 jit_solution(16950787736190679735)
XLA Ops:
  0.6 155.3 %layer_with_copies.1 = (bf16[4,128,768]{2,1,0:T(8,128)(2,1)}, bf16[4,128,768]{2,1,0:T(8,128)(2,1)}, f32[96,192]{1,0:T(8,128)}, f32[96,192]{1,0:T(8,128)}, f32[96...) custom-call(bf16[4,128,768]{2,1,0:T(8,128)(2,1)} %x_in.1, ...), custom_call_target="tpu_custom_call" | custom-call | tf_op jit(solution)/shard_map/layer_with_copies/pallas_call | solution.py:730
  155.9 2.8 %part_outputs.1 = (bf16[4,128,768]{2,1,0:T(8,128)(2,1)}, bf16[4,128,768]{2,1,0:T(8,128)(2,1)}, f32[96,192]{1,0:T(8,128)}, f32[96,192]{1,0:T(8,128)}, f32[96,192]...) custom-call(bf16[4,128,768]{2,1,0:T(8,128)(2,1)} %get-tuple-element., ...), custom_call_target="tpu_custom_call" | custom-call | tf_op jit(solution)/shard_map/part_outputs/pallas_call | solution.py:794

commit v4 on v3

--- a/solution.py
+++ b/solution.py
@@ -171,13 +171,10 @@
     "oz11", "os11", "f02", "oz12", "os12", "oz13", "os13", "b2", "f03",
 )
 THIRD = ()
-ATTEND = {
-    0: ("p11", "z21", "s21", "iz22", "is22", "iz23", "is23"), 1: ("p12", "f10"), 2: ("c", "p20"),
-    3: ("p13",), 4: ("f11", "oz22", "os22"), 5: ("p21", "oz23", "os23"), 6: ("f12",), 7: ("p22", "f13"),
-}
-AFTER_NORM = ("p23", "f20")
+ATTEND = {0: ('p11','z21','s21','iz22','is22','iz23','is23'), 1: ('p12','f10'), 2: ('c',), 3: ('p13',), 4: ('f11','p20'), 5: ('oz22','os22'), 6: ('p21',), 7: ('oz23','os23','f12')}
+AFTER_NORM = ('f13',)
 TURN = {}
-UP = {0: ("f21",), 1: ("f22",), 3: ("f23",)}
+UP = {0:('p22','f20'),1:('p23','f21',),2:('f22',),3:('f23',)}
 AFTER_GRAD_DOWN = ()
 DOWN = {0: ("e20",), 1: ("e21",), 2: ("e22",), 3: ("e23",)}
 UP_BACK = {}
@@ -187,7 +184,8 @@
     7: ("t2", "e01"),
 }
 AFTER_ROWS = ("e02", "e03", "t1")
-LAST = ("l00", "l01", "l02", "r00", "r01", "l03")
+LAST = ("l00", "l01")
+END = ("l02", "r00", "r01", "l03")
 
 
 def block(i):
@@ -690,6 +688,7 @@
     for i in range(1, 8):
         small_copy(i).start()
     take(AFTER_ROWS)
+    take(LAST)
     total = gain_parts[dp]
     for i in range(1, 8):
         small_in(i).wait_recv()
@@ -698,7 +697,7 @@
     for j in range(1, 4):
         q = lax.rem(z + j, 4)
         send(gain_own_sum, small_z.at[z], egzs.at[q], egzr.at[z], (dp, q)).start()
-    take(LAST)
+    take(END)
     for i in range(1, 8):
         other = lax.rem(dp + i, 8)
         send(gain_own, gain_all.at[other], gs.at[other], gr.at[other], (other, z)).wait_send()

time: 160 us -> 157 us (0.981)
  Pallas kernels: 158 us -> 155 us
    pallas_call x1, Pallas kernels: 155 us -> 152 us  [layer(): pl.pallas_call(layer_kernel, out_shape=(jax.ShapeDtypeStruct(x.shape, BF)...]
where the time goes in v4:
time: 157 us; the launch traced here: 156 us
  Pallas kernels  155 us (99%)
    pallas_call x1, Pallas kernels, layer(): pl.pallas_call(layer_kernel, out_shape=(jax.ShapeDtypeStruct(x.shape, BF)...  152 us

profile of v4, /device:TPU:0, one launch (start us, length us, event | category | flops | bytes accessed | tf_op | source)
XLA Modules:
  0.0 156.1 jit_solution(3195205880608466283)
XLA Ops:
  0.6 152.5 %layer_with_copies.1 = (bf16[4,128,768]{2,1,0:T(8,128)(2,1)}, bf16[4,128,768]{2,1,0:T(8,128)(2,1)}, f32[96,192]{1,0:T(8,128)}, f32[96,192]{1,0:T(8,128)}, f32[96...) custom-call(bf16[4,128,768]{2,1,0:T(8,128)(2,1)} %x_in.1, ...), custom_call_target="tpu_custom_call" | custom-call | tf_op jit(solution)/shard_map/layer_with_copies/pallas_call | solution.py:729
  153.1 2.8 %part_outputs.1 = (bf16[4,128,768]{2,1,0:T(8,128)(2,1)}, bf16[4,128,768]{2,1,0:T(8,128)(2,1)}, f32[96,192]{1,0:T(8,128)}, f32[96,192]{1,0:T(8,128)}, f32[96,192]...) custom-call(bf16[4,128,768]{2,1,0:T(8,128)(2,1)} %get-tuple-element., ...), custom_call_target="tpu_custom_call" | custom-call | tf_op jit(solution)/shard_map/part_outputs/pallas_call | solution.py:793

commit v5 on v4

--- a/solution.py
+++ b/solution.py
@@ -183,8 +183,8 @@
     0: ("e10", "e11"), 1: ("e12", "e13", "r20", "r21"), 3: ("l10", "l11"), 5: ("l12", "l13", "r10", "r11", "e00"),
     7: ("t2", "e01"),
 }
-AFTER_ROWS = ("e02", "e03", "t1")
-LAST = ("l00", "l01")
+AFTER_ROWS = ('e02','l00','e03','t1')
+LAST = ('l01',)
 END = ("l02", "r00", "r01", "l03")
 
 
@@ -634,10 +634,19 @@
     loop(4, norm_f_back)
     take(AFTER_NORM_BACK)
 
+    def own_attention(k):
+        q = quarter(k)
+        emit_own(0, k, na_t, act[q, :, 0:640], (ct_t, cb[q]))
+
     def attend_back(i):
         q = quarter(i)
         w = weights[0, q].reshape(D, D)
         dctx = between(natural(nrm[...], w[:, 512:768]), 64, 192).astype(BF)
+
+        @pl.when(i > 0)
+        def _():
+            own_attention(i - 1)
+
         q8, v, k, cx = qb[q], vb[q], kb[q], cb[q]
         dq = jnp.zeros((LEN, 256), F32)
         dk = jnp.zeros((LEN, 256), F32)
@@ -660,7 +669,7 @@
         serve(2 * i, ATTEND_BACK)
         emit_other(0, q, na_t, d, (ct_t, cx))
         add(i, against(d, w[:, 0:640]))
-        emit_own(0, i, na_t, d, (ct_t, cx))
+        act[q, :, 0:640] = d
         serve(2 * i + 1, ATTEND_BACK)
 
     loop(4, attend_back)
@@ -673,6 +682,7 @@
 
     loop(4, norm_a_back)
     rows_start(3, ct_ref, dxs_ref)
+    own_attention(3)
     for i in range(2):
         for p in range(8):
             gain_parts[p, i : i + 1, 0:96] = gain_sum[i : i + 1, 96 * p : 96 * (p + 1)]

time: 157 us -> 155 us (0.987)
  Pallas kernels: 155 us -> 153 us
    pallas_call x1, Pallas kernels: 152 us -> 151 us  [layer(): pl.pallas_call(layer_kernel, out_shape=(jax.ShapeDtypeStruct(x.shape, BF)...]
where the time goes in v5:
time: 155 us; the launch traced here: 154 us
  Pallas kernels  153 us (99%)
    pallas_call x1, Pallas kernels, layer(): pl.pallas_call(layer_kernel, out_shape=(jax.ShapeDtypeStruct(x.shape, BF)...  151 us

profile of v5, /device:TPU:0, one launch (start us, length us, event | category | flops | bytes accessed | tf_op | source)
XLA Modules:
  0.0 154.2 jit_solution(17121871875414871190)
XLA Ops:
  0.6 150.7 %layer_with_copies.1 = (bf16[4,128,768]{2,1,0:T(8,128)(2,1)}, bf16[4,128,768]{2,1,0:T(8,128)(2,1)}, f32[96,192]{1,0:T(8,128)}, f32[96,192]{1,0:T(8,128)}, f32[96...) custom-call(bf16[4,128,768]{2,1,0:T(8,128)(2,1)} %x_in.1, ...), custom_call_target="tpu_custom_call" | custom-call | tf_op jit(solution)/shard_map/layer_with_copies/pallas_call | solution.py:739
  151.3 2.8 %part_outputs.1 = (bf16[4,128,768]{2,1,0:T(8,128)(2,1)}, bf16[4,128,768]{2,1,0:T(8,128)(2,1)}, f32[96,192]{1,0:T(8,128)}, f32[96,192]{1,0:T(8,128)}, f32[96,192]...) custom-call(bf16[4,128,768]{2,1,0:T(8,128)(2,1)} %get-tuple-element., ...), custom_call_target="tpu_custom_call" | custom-call | tf_op jit(solution)/shard_map/part_outputs/pallas_call | solution.py:803

commit v6 on v5

--- a/solution.py
+++ b/solution.py
@@ -171,7 +171,7 @@
     "oz11", "os11", "f02", "oz12", "os12", "oz13", "os13", "b2", "f03",
 )
 THIRD = ()
-ATTEND = {0: ('p11','z21','s21','iz22','is22','iz23','is23'), 1: ('p12','f10'), 2: ('c',), 3: ('p13',), 4: ('f11','p20'), 5: ('oz22','os22'), 6: ('p21',), 7: ('oz23','os23','f12')}
+ATTEND = {0: ('p11','z21','s21','iz22','is22','iz23','is23'), 1: ('p12','f10','c'), 3: ('p13',), 4: ('f11','p20'), 5: ('oz22','os22'), 6: ('p21',), 7: ('oz23','os23','f12')}
 AFTER_NORM = ('f13',)
 TURN = {}
 UP = {0:('p22','f20'),1:('p23','f21',),2:('f22',),3:('f23',)}
@@ -680,8 +680,19 @@
         gain_sum[0:1] += grad_gain[None]
         ct_ref[i] = (mid[block(i)] + back).astype(BF)
 
-    loop(4, norm_a_back)
-    rows_start(3, ct_ref, dxs_ref)
+    def back_and_send(k):
+        q = nearest(z, 3 - k)
+        norm_a_back(q)
+
+        @pl.when(k < 3)
+        def _():
+            send(ct_ref.at[q], dxs_ref.at[z], as_.at[3, q], ar.at[3, z], (dp, q)).start()
+
+        @pl.when(k == 3)
+        def _():
+            pltpu.make_async_copy(ct_ref.at[z], dxs_ref.at[z], local_sem.at[3]).start()
+
+    loop(4, back_and_send)
     own_attention(3)
     for i in range(2):
         for p in range(8):

time: 155 us -> 154 us (level)
  no operation moved by 1% of the time
where the time goes in v6:
time: 154 us
  Pallas kernels  153 us (99%)
    pallas_call x1, Pallas kernels, layer(): pl.pallas_call(layer_kernel, out_shape=(jax.ShapeDtypeStruct(x.shape, BF)...  150 us

profile of v6, /device:TPU:0, one launch (start us, length us, event | category | flops | bytes accessed | tf_op | source)
XLA Modules:
  0.0 154.1 jit_solution(17021966223028321249)
XLA Ops:
  0.6 150.5 %layer_with_copies.1 = (bf16[4,128,768]{2,1,0:T(8,128)(2,1)}, bf16[4,128,768]{2,1,0:T(8,128)(2,1)}, f32[96,192]{1,0:T(8,128)}, f32[96,192]{1,0:T(8,128)}, f32[96...) custom-call(bf16[4,128,768]{2,1,0:T(8,128)(2,1)} %x_in.1, ...), custom_call_target="tpu_custom_call" | custom-call | tf_op jit(solution)/shard_map/layer_with_copies/pallas_call | solution.py:750
  151.1 2.8 %part_outputs.1 = (bf16[4,128,768]{2,1,0:T(8,128)(2,1)}, bf16[4,128,768]{2,1,0:T(8,128)(2,1)}, f32[96,192]{1,0:T(8,128)}, f32[96,192]{1,0:T(8,128)}, f32[96,192]...) custom-call(bf16[4,128,768]{2,1,0:T(8,128)(2,1)} %get-tuple-element., ...), custom_call_target="tpu_custom_call" | custom-call | tf_op jit(solution)/shard_map/part_outputs/pallas_call | solution.py:814
